TPU v7x, 32 devices: a whole 2x2x4 slice. The times are simulated.
32 devices in a mesh: groups: 2 (over x), tm: 16 (over z, y, core).
Axes of the slice: x: 2, y: 2, z: 4, core: 2. Of those that a mesh axis runs over, the one named last changes fastest.
Arguments:
- perambulator: bfloat16 [64, 768, 1536], P('groups', 'tm'), parts along dimension 0, may hold values from -6 to 6
- elementals: bfloat16 [32, 16, 192, 384], P(('groups', 'tm')), parts along dimension 0, may hold values from -0.3125 to 0.3125
- diagrams: int32 [32, 3, 2], P('tm'), may hold values from 0 to 15
- counts: int32 [32], P('tm'), may hold values from 1 to 3, as said below
Outputs:
- correlator: float32 [64, 3, 2], P(('groups', 'tm')), parts along dimension 0
There are 2 independent parts, one for each index of `groups`. A program takes and returns all parts, laid end to end along the dimension named above; an argument that names none is the same for every part. Nothing has to cross between parts.
Inputs may be any that keep to these rules, and one draw needn't show every extreme that they name: `counts`: each pair lists 1 to 3 diagrams; in every draw some pair lists exactly 3. `diagrams`: slots at or beyond a pair's count are ignored.
All inputs are finite; a program needn't handle non-finite values.
Results may differ from a plain program's by a relative error of at most 0.0029.
Values may be sent and summed in bfloat16 or wider, within the bound.
No kernel may reach another device: no remote copies, remote signals or barrier semaphores. Data moves between devices by JAX's collectives and lax.ppermute only.
A program may use at most 128 MiB of HBM per device.

v0:
```python
import functools

import jax
import jax.numpy as jnp
from jax import lax
from jax.experimental import pallas as pl
from jax.experimental.pallas import tpu as pltpu
from jax.sharding import PartitionSpec as P

NT_DIMS = (((1,), (1,)), ((), ()))


def exchanged(x, mask):
    devices = lax.axis_size("tm")
    return lax.ppermute(x, "tm", [(i, i ^ mask) for i in range(devices)])


def passed_along(x, by, mask=0):
    devices = lax.axis_size("tm")
    return lax.ppermute(x, "tm", [(i, ((i + by) % devices) ^ mask) for i in range(devices)])


def halves_swapped(x):
    vectors = x.shape[1] // 2
    return jnp.concatenate([x[:, vectors:], x[:, :vectors]], axis=1)


def pair_kernel(slot, count_ref, tau_ref, sink_ref, source_ref, out_ref, tile_ref, swap_ref, left_ref):
    slots = sink_ref.shape[0]
    rows, packed = tile_ref.shape
    vectors = packed // 2
    blocks = rows // vectors
    first_half = lax.broadcasted_iota(jnp.int32, (vectors, packed), 1) < vectors

    @pl.when(pl.program_id(0) == 0)
    def _():
        for d in range(slots):
            out_ref[d, 0] = 0.0
            out_ref[d, 1] = 0.0

    for b in range(blocks):
        tile = tau_ref[:, 0, :, b * packed : (b + 1) * packed].reshape(vectors, packed)
        tile_ref[b * vectors : (b + 1) * vectors, :] = tile
        part = halves_swapped(tile)
        swap_ref[b * vectors : (b + 1) * vectors, :] = jnp.where(first_half, -part, part)

    for d in range(slots):

        @pl.when(d < count_ref[slot])
        def _():
            sink = sink_ref[d]
            embedding = jnp.concatenate(
                [jnp.where(first_half, sink, -sink), halves_swapped(sink)], axis=0
            )
            left_ref[...] = lax.dot_general(
                tile_ref[...], embedding, NT_DIMS, preferred_element_type=jnp.float32
            ).astype(jnp.bfloat16)

            def joined(ref):
                return jnp.concatenate(
                    [ref[b * vectors : (b + 1) * vectors, :] for b in range(blocks)], axis=1
                )

            left = joined(left_ref)
            block_real = lax.dot_general(
                left, joined(tile_ref), NT_DIMS, preferred_element_type=jnp.float32
            )
            block_imag = lax.dot_general(
                left, joined(swap_ref), NT_DIMS, preferred_element_type=jnp.float32
            )
            source = source_ref[0, d].astype(jnp.float32)
            real = source[:, :vectors]
            imag = source[:, vectors:]
            out_ref[d, 0] += jnp.sum(real * block_real - imag * block_imag)
            out_ref[d, 1] += jnp.sum(real * block_imag + imag * block_real)


def pair_sums(tau, slot, sinks, sources, counts):
    slots, vectors, packed = sinks.shape
    spins = tau.shape[0] * tau.shape[2] // vectors
    layer, columns, width = tau.shape[0] // spins, tau.shape[2], tau.shape[3]
    smem = pl.BlockSpec(memory_space=pltpu.SMEM)
    flops = 4 * spins * slots * width * vectors * packed
    moved = 2 * (spins * vectors * width + 2 * slots * vectors * packed)
    rows = vectors * width // packed
    return pl.pallas_call(
        functools.partial(pair_kernel, slot),
        grid=(spins,),
        in_specs=[
            smem,
            pl.BlockSpec((layer, 1, columns, width), lambda s: (s, slot, 0, 0)),
            pl.BlockSpec((slots, vectors, packed), lambda s: (0, 0, 0)),
            pl.BlockSpec((1, slots, vectors, packed), lambda s: (slot, 0, 0, 0)),
        ],
        out_specs=smem,
        out_shape=jax.ShapeDtypeStruct((slots, 2), jnp.float32),
        scratch_shapes=[pltpu.VMEM((rows, packed), jnp.bfloat16)] * 3,
        compiler_params=pltpu.CompilerParams(vmem_limit_bytes=32 * 1024 * 1024),
        cost_estimate=pl.CostEstimate(flops=flops, bytes_accessed=moved, transcendentals=0),
    )(counts, tau, sinks, sources)


def body(perambulator, elementals, diagrams, counts):
    devices = lax.axis_size("tm")
    me = lax.axis_index("tm")
    pair_count, slots = diagrams.shape[:2]
    columns, width = perambulator.shape[1:]
    vectors, packed = elementals.shape[2:]
    half = devices // 2
    own_set = elementals[0]
    high = (me >= half).astype(jnp.int32)
    halves = [list(range(half)), list(range(half, devices))]

    def regrouped(which):
        sent = lax.dynamic_index_in_dim(grouped, which, 0, keepdims=False)
        tau = lax.all_to_all(
            sent, "tm", split_axis=0, concat_axis=0, axis_index_groups=halves, tiled=True
        )
        if columns % 16 != 0:
            tau = jnp.moveaxis(tau, 1, 0).reshape(pair_count, -1, vectors, width)
            tau = jnp.moveaxis(tau, 0, 1)
        return tau

    grouped = perambulator.reshape(2, half, pair_count, columns, width)
    given_tau = regrouped(1 - high)
    given_counts = exchanged(counts, half)
    own_sources = jnp.take(own_set, diagrams[:, :, 1].reshape(-1), axis=0, mode="clip")
    given_sources = exchanged(own_sources, half).reshape(pair_count, slots, vectors, packed)
    own_sources = own_sources.reshape(pair_count, slots, vectors, packed)
    chosen = []
    for slot in range(pair_count):
        by = (slot + 1) * devices // (pair_count + 1)
        wanted = passed_along(diagrams[slot, :, 0], by)
        chosen.append((by, jnp.take(own_set, wanted, axis=0, mode="clip")))
    given_sinks = [passed_along(sets, -by, half) for by, sets in chosen]
    own_sinks = [passed_along(sets, -by) for by, sets in chosen]
    own_tau = regrouped(high)

    def sums(tau, sinks, sources, counts):
        return jnp.stack(
            [pair_sums(tau, slot, sinks[slot], sources, counts) for slot in range(pair_count)]
        )

    given = sums(given_tau, given_sinks, given_sources, given_counts)
    given, counts = lax.optimization_barrier((given, counts))
    got = exchanged(given, half)
    kept = sums(own_tau, own_sinks, own_sources, counts)
    return (kept + got) / (columns * devices)


def solution(mesh):
    return jax.shard_map(
        body,
        mesh=mesh,
        in_specs=(
            P("groups", "tm", None),
            P(("groups", "tm"), None, None, None),
            P("tm", None, None),
            P("tm"),
        ),
        out_specs=P(("groups", "tm"), None, None),
        check_vma=False,
    )
```

profile of v0, /device:TPU:0, one launch (start us, length us, event | category | flops | bytes accessed | tf_op | source)
XLA Modules:
  0.0 163.4 jit_solution(12775013640918085389)
XLA Ops:
  0.0 0.0 copy-start
  0.0 4.4 %dynamic-slice_bitcast_fusion = (bf16[8,2,48,1536]{3,2,1,0:T(8,128)(2,1)}, bf16[8,2,48,1536]{3,2,1,0:T(8,128)(2,1)S(1)}) fusion(bf16[2,8,2,48,1536]{4,3,2,1,0:T(8,128)(2,1)} %bitcast.21, s32[]{:T(128)S(6)} %select_n.8, s32[]{:T(128)S(6)} %select_n.7), kind=kLoop, calls=%fused_computation.3 | loop fusion | bytes 9437192 | tf_op jit(solution)/shard_map/jit(dynamic_index_in_dim)/squeeze | solution.py:115
  4.4 34.0 %all_to_all.10.tau_ref = bf16[8,2,48,1536]{3,2,1,0:T(8,128)(2,1)} all-to-all(bf16[8,2,48,1536]{3,2,1,0:T(8,128)(2,1)S(1)} %get-tuple-element.10), channel_id=1, replica_groups={{0,1,2,3,4,5,6,7},{8,9,10,11,12,13,14,15},{16,17,18,19,20,21,22,23},{24..., dimensions={0} | all-to-all | bytes 4718592 | tf_op jit(solution)/shard_map/all_to_all | solution.py:116
  38.4 0.0 copy-start.3
  38.4 4.5 %all-to-all-start.1 = ((bf16[8,2,48,1536]{3,2,1,0:T(8,128)(2,1)}), bf16[8,2,48,1536]{3,2,1,0:T(8,128)(2,1)}, u32[]{:S(2)}, u32[]{:S(2)}) async-start(bf16[8,2,48,1536]{3,2,1,0:T(8,128)(2,1)} %get-tuple-element.9), calls=%async_computation.1 | async-start | bytes 4718592 | tf_op jit(solution)/shard_map/all_to_all | solution.py:116
  42.9 0.0 copy-done.3
  43.0 0.0 copy-start.2
  43.0 0.1 reshape.23
  43.1 0.0 copy-done
  43.1 0.7 gather_fusion.1
  43.8 2.7 %collective-permute-start.3 = (bf16[6,192,384]{2,1,0:T(8,128)(2,1)S(1)}, bf16[6,192,384]{2,1,0:T(8,128)(2,1)}, u32[]{:S(2)}, u32[]{:S(2)}) collective-permute-start(bf16[6,192,384]{2,1,0:T(8,128)(2,1)S(1)} %gather_fusion.1), channel_id=1, source_target_pairs={{0,8},{1,9},{2,10},{3,11},{4,12},{5,13},{6,14},{7,15},{8,0},{9,1},... | collective-permute-start | bytes 2654216 | tf_op jit(solution)/shard_map/ppermute | solution.py:15
  46.5 1.4 collective-permute-start.1
  47.9 40.4 %collective-permute-done.1 = s32[3]{0:T(128)S(1)} collective-permute-done((s32[3]{0:T(128)S(1)}, s32[3]{0:T(128)S(1)}, u32[]{:S(2)}, u32[]{:S(2)}) %collective-permute-start.1) | collective-permute-done | bytes 44 | tf_op jit(solution)/shard_map/ppermute | solution.py:20
  88.3 1.4 gather_fusion
  89.7 5.0 %collective-permute-start.2 = (bf16[3,192,384]{2,1,0:T(8,128)(2,1)}, bf16[3,192,384]{2,1,0:T(8,128)(2,1)}, u32[]{:S(2)}, u32[]{:S(2)}) collective-permute-start(bf16[3,192,384]{2,1,0:T(8,128)(2,1)} %gather_fusion), channel_id=1, source_target_pairs={{0,3},{1,4},{2,5},{3,6},{4,7},{5,8},{6,9},{7,10},{8,11},{9,12},{10... | collective-permute-start | bytes 1327112 | tf_op jit(solution)/shard_map/ppermute | solution.py:20
  94.6 0.7 collective-permute-start.4
  95.4 3.7 %collective-permute-done.4 = s32[3]{0:T(128)S(1)} collective-permute-done((s32[3]{0:T(128)S(1)}, s32[3]{0:T(128)S(1)}, u32[]{:S(2)}, u32[]{:S(2)}) %collective-permute-start.4) | collective-permute-done | bytes 44 | tf_op jit(solution)/shard_map/ppermute | solution.py:20
  99.1 1.4 gather_fusion.2
  100.5 9.2 %collective-permute-start.5 = (bf16[3,192,384]{2,1,0:T(8,128)(2,1)}, bf16[3,192,384]{2,1,0:T(8,128)(2,1)S(1)}, u32[]{:S(2)}, u32[]{:S(2)}) collective-permute-start(bf16[3,192,384]{2,1,0:T(8,128)(2,1)} %gather_fusion.2), channel_id=1, source_target_pairs={{0,14},{1,15},{2,0},{3,1},{4,2},{5,3},{6,4},{7,5},{8,6},{9,7},{10,... | collective-permute-start | bytes 1327112 | tf_op jit(solution)/shard_map/ppermute | solution.py:20
  109.7 0.0 copy-done.2
  109.7 0.9 collective-permute-start
  110.6 0.2 collective-permute-start.6
  110.8 11.4 %collective-permute-done.count_ref = s32[2]{0:T(128)S(1)} collective-permute-done((s32[2]{0:T(128)S(1)}, s32[2]{0:T(128)S(1)}, u32[]{:S(2)}, u32[]{:S(2)}) %collective-permute-start) | collective-permute-done | bytes 40 | tf_op jit(solution)/shard_map/ppermute | solution.py:15
  122.3 0.0 collective-permute-start.7
  122.3 0.0 collective-permute-done.2.sink_ref
  122.3 0.0 collective-permute-done.3
  122.3 0.0 copy-start.1
  122.3 1.7 %copy-done.1 = bf16[8,2,48,1536]{3,2,1,0:T(8,128)(2,1)S(1)} copy-done((bf16[8,2,48,1536]{3,2,1,0:T(8,128)(2,1)S(1)}, bf16[8,2,48,1536]{3,2,1,0:T(8,128)(2,1)}, u32[]{:S(2)}) %copy-start.1) | copy-done | bytes 2359320
  123.9 9.7 %shard_map.46 = f32[3,2]{1,0:T(4,128)S(1)} custom-call(s32[2]{0:T(128)S(1)} %collective-permute-done.count_ref, bf16[8,2,48,1536]{3,2,1,0:T(8,128)(2,1)S(1)} %copy-done.1, bf16[3,192,384]{2,1,0:T(8,128)(2,1)} %collective-permute-done.2.sink_ref, bf16[2,3,192,384]{3,2,1,0:T(8,128)(2,1)} %bitcast.4.source_ref), custom_call_target="tpu_custom_call" | custom-call | flops 2717908992 | bytes 2064384 | tf_op jit(solution)/shard_map/pallas_call | solution.py:86
  133.7 0.0 collective-permute-done.5.sink_ref
  133.7 4.7 %shard_map.47 = f32[3,2]{1,0:T(4,128)S(1)} custom-call(s32[2]{0:T(128)S(1)} %collective-permute-done.count_ref, bf16[8,2,48,1536]{3,2,1,0:T(8,128)(2,1)S(1)} %copy-done.1, bf16[3,192,384]{2,1,0:T(8,128)(2,1)S(1)} %collective-permute-done.5.sink_ref, bf16[2,3,192,384]{3,2,1,0:T(8,128)(2,1)} %bitcast.4.source_ref), custom_call_target="tpu_custom_call" | custom-call | flops 2717908992 | bytes 2064384 | tf_op jit(solution)/shard_map/pallas_call | solution.py:86
  138.4 0.1 copy.9
  138.5 0.1 copy.10
  138.6 0.0 collective-permute-done.6.sink_ref
  138.6 0.0 all-to-all-done.1.tau_ref
  138.6 4.9 %shard_map.48 = f32[3,2]{1,0:T(4,128)S(1)} custom-call(s32[2]{0:T(128)S(1)} %copy-done.2, bf16[8,2,48,1536]{3,2,1,0:T(8,128)(2,1)} %all-to-all-done.1.tau_ref, bf16[3,192,384]{2,1,0:T(8,128)(2,1)} %collective-permute-done.6.sink_ref, bf16[2,3,192,384]{3,2,1,0:T(8,128)(2,1)S(1)} %bitcast.19), custom_call_target="tpu_custom_call" | custom-call | flops 2717908992 | bytes 2064384 | tf_op jit(solution)/shard_map/pallas_call | solution.py:86
  143.5 0.1 copy.11
  143.6 0.0 collective-permute-done.7.sink_ref
  143.6 9.9 %shard_map.49 = f32[3,2]{1,0:T(4,128)S(1)} custom-call(s32[2]{0:T(128)S(1)} %copy-done.2, bf16[8,2,48,1536]{3,2,1,0:T(8,128)(2,1)} %all-to-all-done.1.tau_ref, bf16[3,192,384]{2,1,0:T(8,128)(2,1)} %collective-permute-done.7.sink_ref, bf16[2,3,192,384]{3,2,1,0:T(8,128)(2,1)S(1)} %bitcast.20), custom_call_target="tpu_custom_call" | custom-call | flops 2717908992 | bytes 2064384 | tf_op jit(solution)/shard_map/pallas_call | solution.py:86
  153.4 0.1 copy.12
  153.5 7.7 %collective-permute-start.8 = (f32[2,3,2]{1,2,0:T(2,128)S(1)}, f32[2,3,2]{1,2,0:T(2,128)S(1)}, u32[]{:S(2)}, u32[]{:S(2)}) collective-permute-start(f32[2,3,2]{1,2,0:T(2,128)S(1)} %pad_maximum_fusion), channel_id=1, source_target_pairs={{0,8},{1,9},{2,10},{3,11},{4,12},{5,13},{6,14},{7,15},{8,0},{9,1},... | collective-permute-start | bytes 152 | tf_op jit(solution)/shard_map/ppermute | solution.py:15
  161.2 1.6 collective-permute-done.8
  162.8 0.6 fusion
  (6 shorter events, 0.0 us)
Async XLA Ops:
  0.0 43.1 %copy-start = (bf16[1,16,192,384]{3,2,1,0:T(8,128)(2,1)S(1)}, bf16[1,16,192,384]{3,2,1,0:T(8,128)(2,1)}, u32[]{:S(2)}) copy-start(bf16[1,16,192,384]{3,2,1,0:T(8,128)(2,1)} %param.5) | copy-start | bytes 7077892
  38.4 4.5 %copy-start.3 = (s32[2,3,2]{1,2,0:T(2,128)S(1)}, s32[2,3,2]{1,2,0:T(2,128)}, u32[]{:S(2)}) copy-start(s32[2,3,2]{1,2,0:T(2,128)} %param.6) | copy-start | bytes 148
  38.4 100.2 %all-to-all-start.1 = ((bf16[8,2,48,1536]{3,2,1,0:T(8,128)(2,1)}), bf16[8,2,48,1536]{3,2,1,0:T(8,128)(2,1)}, u32[]{:S(2)}, u32[]{:S(2)}) async-start(bf16[8,2,48,1536]{3,2,1,0:T(8,128)(2,1)} %get-tuple-element.9), calls=%async_computation.1 | async-start | bytes 4718592 | tf_op jit(solution)/shard_map/all_to_all | solution.py:116
  43.0 66.8 %copy-start.2 = (s32[2]{0:T(128)S(1)}, s32[2]{0:T(128)}, u32[]{:S(2)}) copy-start(s32[2]{0:T(128)} %count_ref.1) | copy-start | bytes 28
  43.8 78.4 %collective-permute-start.3 = (bf16[6,192,384]{2,1,0:T(8,128)(2,1)S(1)}, bf16[6,192,384]{2,1,0:T(8,128)(2,1)}, u32[]{:S(2)}, u32[]{:S(2)}) collective-permute-start(bf16[6,192,384]{2,1,0:T(8,128)(2,1)S(1)} %gather_fusion.1), channel_id=1, source_target_pairs={{0,8},{1,9},{2,10},{3,11},{4,12},{5,13},{6,14},{7,15},{8,0},{9,1},... | collective-permute-start | bytes 2654216 | tf_op jit(solution)/shard_map/ppermute | solution.py:15
  46.5 41.8 %collective-permute-start.1 = (s32[3]{0:T(128)S(1)}, s32[3]{0:T(128)S(1)}, u32[]{:S(2)}, u32[]{:S(2)}) collective-permute-start(s32[3]{0:T(128)S(1)} %get-tuple-element.11), channel_id=1, source_target_pairs={{0,5},{1,6},{2,7},{3,8},{4,9},{5,10},{6,11},{7,12},{8,13},{9,14},{... | collective-permute-start | bytes 44 | tf_op jit(solution)/shard_map/ppermute | solution.py:20
  89.7 32.6 %collective-permute-start.2 = (bf16[3,192,384]{2,1,0:T(8,128)(2,1)}, bf16[3,192,384]{2,1,0:T(8,128)(2,1)}, u32[]{:S(2)}, u32[]{:S(2)}) collective-permute-start(bf16[3,192,384]{2,1,0:T(8,128)(2,1)} %gather_fusion), channel_id=1, source_target_pairs={{0,3},{1,4},{2,5},{3,6},{4,7},{5,8},{6,9},{7,10},{8,11},{9,12},{10... | collective-permute-start | bytes 1327112 | tf_op jit(solution)/shard_map/ppermute | solution.py:20
  94.6 4.4 %collective-permute-start.4 = (s32[3]{0:T(128)S(1)}, s32[3]{0:T(128)S(1)}, u32[]{:S(2)}, u32[]{:S(2)}) collective-permute-start(s32[3]{0:T(128)S(1)} %get-tuple-element.12), channel_id=1, source_target_pairs={{0,10},{1,11},{2,12},{3,13},{4,14},{5,15},{6,0},{7,1},{8,2},{9,3},... | collective-permute-start | bytes 44 | tf_op jit(solution)/shard_map/ppermute | solution.py:20
  100.5 33.1 %collective-permute-start.5 = (bf16[3,192,384]{2,1,0:T(8,128)(2,1)}, bf16[3,192,384]{2,1,0:T(8,128)(2,1)S(1)}, u32[]{:S(2)}, u32[]{:S(2)}) collective-permute-start(bf16[3,192,384]{2,1,0:T(8,128)(2,1)} %gather_fusion.2), channel_id=1, source_target_pairs={{0,14},{1,15},{2,0},{3,1},{4,2},{5,3},{6,4},{7,5},{8,6},{9,7},{10,... | collective-permute-start | bytes 1327112 | tf_op jit(solution)/shard_map/ppermute | solution.py:20
  109.7 12.5 %collective-permute-start = (s32[2]{0:T(128)S(1)}, s32[2]{0:T(128)S(1)}, u32[]{:S(2)}, u32[]{:S(2)}) collective-permute-start(s32[2]{0:T(128)S(1)} %copy-done.2), channel_id=1, source_target_pairs={{0,8},{1,9},{2,10},{3,11},{4,12},{5,13},{6,14},{7,15},{8,0},{9,1},... | collective-permute-start | bytes 32 | tf_op jit(solution)/shard_map/ppermute | solution.py:15
  110.6 28.0 %collective-permute-start.6 = (bf16[3,192,384]{2,1,0:T(8,128)(2,1)}, bf16[3,192,384]{2,1,0:T(8,128)(2,1)}, u32[]{:S(2)}, u32[]{:S(2)}) collective-permute-start(bf16[3,192,384]{2,1,0:T(8,128)(2,1)} %gather_fusion), channel_id=1, source_target_pairs={{0,11},{1,12},{2,13},{3,14},{4,15},{5,0},{6,1},{7,2},{8,3},{9,4},{... | collective-permute-start | bytes 1327112 | tf_op jit(solution)/shard_map/ppermute | solution.py:20
  122.3 21.3 %collective-permute-start.7 = (bf16[3,192,384]{2,1,0:T(8,128)(2,1)}, bf16[3,192,384]{2,1,0:T(8,128)(2,1)}, u32[]{:S(2)}, u32[]{:S(2)}) collective-permute-start(bf16[3,192,384]{2,1,0:T(8,128)(2,1)} %gather_fusion.2), channel_id=1, source_target_pairs={{0,6},{1,7},{2,8},{3,9},{4,10},{5,11},{6,12},{7,13},{8,14},{9,15},... | collective-permute-start | bytes 1327112 | tf_op jit(solution)/shard_map/ppermute | solution.py:20
  122.3 1.7 %copy-start.1 = (bf16[8,2,48,1536]{3,2,1,0:T(8,128)(2,1)S(1)}, bf16[8,2,48,1536]{3,2,1,0:T(8,128)(2,1)}, u32[]{:S(2)}) copy-start(bf16[8,2,48,1536]{3,2,1,0:T(8,128)(2,1)} %all_to_all.10.tau_ref) | copy-start | bytes 7077892
  153.5 9.3 %collective-permute-start.8 = (f32[2,3,2]{1,2,0:T(2,128)S(1)}, f32[2,3,2]{1,2,0:T(2,128)S(1)}, u32[]{:S(2)}, u32[]{:S(2)}) collective-permute-start(f32[2,3,2]{1,2,0:T(2,128)S(1)} %pad_maximum_fusion), channel_id=1, source_target_pairs={{0,8},{1,9},{2,10},{3,11},{4,12},{5,13},{6,14},{7,15},{8,0},{9,1},... | collective-permute-start | bytes 152 | tf_op jit(solution)/shard_map/ppermute | solution.py:15
where the time goes:
time: 165 us; the launch traced here: 163 us
  waiting for transfers between devices  57.1 us (35%)
  blocking collectives  34 us (21%)
  starting transfers between devices  32.2 us (20%)
  Pallas kernels  29.2 us (18%)
  local copies, waits for them, and re-layouts  10.2 us (6%)
    ppermute x6, waiting for transfers between devices, passed_along(): lax.ppermute(x, 'tm', [(i, (i + by) % devices ^ mask) for i in range(devi...  44.1 us
    all_to_all x1, blocking collectives, regrouped(): lax.all_to_all(sent, 'tm', split_axis=0, concat_axis=0, axis_index_groups...  34 us
    pallas_call x4, Pallas kernels, pair_sums(): pl.pallas_call(functools.partial(pair_kernel, slot), grid=(spins,), in_sp...  29.2 us
    ppermute x6, starting transfers between devices, passed_along(): lax.ppermute(x, 'tm', [(i, (i + by) % devices ^ mask) for i in range(devi...  16.5 us
    ppermute x3, waiting for transfers between devices, exchanged(): return lax.ppermute(x, 'tm', [(i, i ^ mask) for i in range(devices)])  13 us
    ppermute x3, starting transfers between devices, exchanged(): return lax.ppermute(x, 'tm', [(i, i ^ mask) for i in range(devices)])  11.3 us
    all_to_all x1, starting transfers between devices, regrouped(): lax.all_to_all(sent, 'tm', split_axis=0, concat_axis=0, axis_index_groups...  4.49 us
    squeeze x1, local copies, waits for them, and re-layouts, regrouped(): sent = lax.dynamic_index_in_dim(grouped, which, 0, keepdims=False)  4.43 us
  transfers between devices with their start and end apart: 10, of which 4 were waited for; matrix products, arithmetic and copies ran while one was open for 2% of the time, Pallas kernels for 12%

commit v1 on v0

v1 whole, which is shorter than its diff:
```python
import functools

import jax
import jax.numpy as jnp
from jax import lax
from jax.experimental import pallas as pl
from jax.experimental.pallas import tpu as pltpu
from jax.sharding import PartitionSpec as P

NT_DIMS = (((1,), (1,)), ((), ()))
ANYWHERE = pl.BlockSpec(memory_space=pl.ANY)
SMEM = pl.BlockSpec(memory_space=pltpu.SMEM)


def exchanged(x, mask):
    devices = lax.axis_size("tm")
    return lax.ppermute(x, "tm", [(i, i ^ mask) for i in range(devices)])


def passed_along(x, by, mask=0):
    devices = lax.axis_size("tm")
    return lax.ppermute(x, "tm", [(i, ((i + by) % devices) ^ mask) for i in range(devices)])


def regroup_kernel(high_ref, source_ref, *refs):
    out_ref, sems = refs[-2:]
    high = high_ref[0]
    copies = []
    for j in range(source_ref.shape[1]):
        for side in range(2):
            which = 1 - high if side == 0 else high
            copies.append(
                pltpu.make_async_copy(
                    source_ref.at[which, j], out_ref.at[j, side], sems.at[2 * j + side]
                )
            )
    for copy in copies:
        copy.start()
    for copy in copies:
        copy.wait()


def regrouped(perambulator, high, half, pair_count, *earlier):
    columns, width = perambulator.shape[1:]
    source = perambulator.reshape(2, half, pair_count, columns, width)
    return pl.pallas_call(
        regroup_kernel,
        in_specs=[SMEM, ANYWHERE] + [ANYWHERE] * len(earlier),
        out_specs=ANYWHERE,
        out_shape=jax.ShapeDtypeStruct((half, 2, pair_count, columns, width), perambulator.dtype),
        scratch_shapes=[pltpu.SemaphoreType.DMA((2 * half,))],
    )(high.reshape(1), source, *earlier)


def halves_swapped(x):
    vectors = x.shape[1] // 2
    return jnp.concatenate([x[:, vectors:], x[:, :vectors]], axis=1)


def pairs_kernel(pair_count, counts_ref, tau_ref, *refs):
    sink_refs = refs[: 2 * pair_count]
    source_refs = refs[2 * pair_count : 2 * pair_count + 2]
    out_ref, sinks, sources, swap_ref, left_ref, sink_sems, source_sems = refs[-7:]
    slots, vectors, packed = sinks.shape[1:]
    spins, _, width = swap_ref.shape
    blocks = width // packed
    pieces = tau_ref.shape[0] // spins
    pair = pl.program_id(0)
    first_half = lax.broadcasted_iota(jnp.int32, (vectors, packed), 1) < vectors

    @pl.when(pair == 0)
    def _():
        for p in range(2 * pair_count):
            side, slot = divmod(p, pair_count)
            for d in range(slots):
                out_ref[p, d, 0] = 0.0
                out_ref[p, d, 1] = 0.0

                @pl.when(d < counts_ref[p])
                def _():
                    pltpu.make_async_copy(
                        sink_refs[p].at[d], sinks.at[p, d], sink_sems.at[p, d]
                    ).start()
                    pltpu.make_async_copy(
                        source_refs[side].at[slot, d], sources.at[p, d], source_sems.at[p, d]
                    ).start()

    def tile(s):
        return tau_ref[s * pieces : (s + 1) * pieces, 0].reshape(vectors, width)

    def part(x, b):
        return x[:, b * packed : (b + 1) * packed]

    for s in range(spins):
        for b in range(blocks):
            swapped = halves_swapped(part(tile(s), b))
            swap_ref[s, :, b * packed : (b + 1) * packed] = jnp.where(
                first_half, -swapped, swapped
            )

    @pl.loop(0, counts_ref[pair])
    def _(d):
        pltpu.make_async_copy(
            sink_refs[0].at[0], sinks.at[pair, d], sink_sems.at[pair, d]
        ).wait()
        sink = sinks[pair, d]
        embedding = jnp.concatenate(
            [jnp.where(first_half, sink, -sink), halves_swapped(sink)], axis=0
        )
        block_real = jnp.zeros((vectors, vectors), jnp.float32)
        block_imag = jnp.zeros((vectors, vectors), jnp.float32)
        for s in range(spins):
            stacked = jnp.concatenate([part(tile(s), b) for b in range(blocks)], axis=0)
            left = lax.dot_general(
                stacked, embedding, NT_DIMS, preferred_element_type=jnp.float32
            ).astype(jnp.bfloat16)
            for b in range(blocks):
                left_ref[s, :, b * packed : (b + 1) * packed] = left[
                    b * vectors : (b + 1) * vectors
                ]
        for s in range(spins):
            block_real += lax.dot_general(
                left_ref[s], tile(s), NT_DIMS, preferred_element_type=jnp.float32
            )
            block_imag += lax.dot_general(
                left_ref[s], swap_ref[s], NT_DIMS, preferred_element_type=jnp.float32
            )
        pltpu.make_async_copy(
            source_refs[0].at[0, 0], sources.at[pair, d], source_sems.at[pair, d]
        ).wait()
        source = sources[pair, d].astype(jnp.float32)
        real = source[:, :vectors]
        imag = source[:, vectors:]
        out_ref[pair, d, 0] = jnp.sum(real * block_real - imag * block_imag)
        out_ref[pair, d, 1] = jnp.sum(real * block_imag + imag * block_real)


def pairs_sums(tau, sinks, sources, counts):
    pairs = len(sinks)
    slots, vectors, packed = sinks[0].shape
    pieces, _, columns, width = tau.shape
    spins = pieces * columns // vectors
    flops = 4 * pairs * spins * slots * width * vectors * packed
    moved = 2 * pairs * (spins * vectors * width + 2 * slots * vectors * packed)
    return pl.pallas_call(
        functools.partial(pairs_kernel, pairs // 2),
        grid=(pairs,),
        in_specs=[SMEM, pl.BlockSpec((pieces, 1, columns, width), lambda p: (0, p, 0, 0))]
        + [ANYWHERE] * (pairs + 2),
        out_specs=SMEM,
        out_shape=jax.ShapeDtypeStruct((pairs, slots, 2), jnp.float32),
        scratch_shapes=[
            pltpu.VMEM((pairs, slots, vectors, packed), jnp.bfloat16),
            pltpu.VMEM((pairs, slots, vectors, packed), jnp.bfloat16),
            pltpu.VMEM((spins, vectors, width), jnp.bfloat16),
            pltpu.VMEM((spins, vectors, width), jnp.bfloat16),
            pltpu.SemaphoreType.DMA((pairs, slots)),
            pltpu.SemaphoreType.DMA((pairs, slots)),
        ],
        compiler_params=pltpu.CompilerParams(vmem_limit_bytes=40 * 1024 * 1024),
        cost_estimate=pl.CostEstimate(flops=flops, bytes_accessed=moved, transcendentals=0),
    )(counts, tau, *sinks, *sources)


def body(perambulator, elementals, diagrams, counts):
    devices = lax.axis_size("tm")
    me = lax.axis_index("tm")
    pair_count, slots = diagrams.shape[:2]
    columns, width = perambulator.shape[1:]
    vectors, packed = elementals.shape[2:]
    half = devices // 2
    own_set = elementals[0]
    high = (me >= half).astype(jnp.int32)
    halves = [list(range(half)), list(range(half, devices))]

    steps = [(slot + 1) * devices // (pair_count + 1) for slot in range(pair_count)]
    wanted = [passed_along(diagrams[slot, :, 0], by) for slot, by in enumerate(steps)]
    given_counts = exchanged(counts, half)
    own_sources = jnp.take(own_set, diagrams[:, :, 1].reshape(-1), axis=0, mode="clip")
    own_sources = own_sources.reshape(pair_count, slots, vectors, packed)
    given_sources = exchanged(own_sources, half)
    chosen = [jnp.take(own_set, index, axis=0, mode="clip") for index in wanted]
    given_sinks = [passed_along(sets, -by, half) for by, sets in zip(steps, chosen)]
    own_sinks = [passed_along(sets, -by) for by, sets in zip(steps, chosen)]

    tau = lax.all_to_all(
        regrouped(perambulator, high, half, pair_count, given_counts, *wanted),
        "tm",
        split_axis=0,
        concat_axis=0,
        axis_index_groups=halves,
        tiled=True,
    ).reshape(half, 2 * pair_count, columns, width)
    if columns % 16 != 0:
        tau = jnp.moveaxis(tau, 1, 0).reshape(2 * pair_count, -1, vectors, width)
        tau = jnp.moveaxis(tau, 0, 1)

    sums = pairs_sums(
        tau,
        given_sinks + own_sinks,
        (given_sources, own_sources),
        jnp.concatenate([given_counts, counts]),
    )
    got = exchanged(sums[:pair_count], half)
    return (sums[pair_count:] + got) / (columns * devices)


def solution(mesh):
    return jax.shard_map(
        body,
        mesh=mesh,
        in_specs=(
            P("groups", "tm", None),
            P(("groups", "tm"), None, None, None),
            P("tm", None, None),
            P("tm"),
        ),
        out_specs=P(("groups", "tm"), None, None),
        check_vma=False,
    )
```

time: 165 us -> 297 us (1.80)
  the two profiles are of different devices: /device:TPU:0 before, /device:TPU:1 now
where the time goes in v1:
time: 297 us; the launch traced here: 299 us
  Pallas kernels  167 us (56%)
  waiting for transfers between devices  100 us (34%)
  starting transfers between devices  20.8 us (7%)
  local copies, waits for them, and re-layouts  11 us (4%)
    pallas_call x1, Pallas kernels, regrouped(): pl.pallas_call(regroup_kernel, in_specs=[SMEM, ANYWHERE] + [ANYWHERE] * l...  144 us
    ppermute x6, waiting for transfers between devices, passed_along(): lax.ppermute(x, 'tm', [(i, (i + by) % devices ^ mask) for i in range(devi...  95.8 us
    pallas_call x1, Pallas kernels, pairs_sums(): pl.pallas_call(functools.partial(pairs_kernel, pairs // 2), grid=(pairs,)...  22.4 us
    ppermute x6, starting transfers between devices, passed_along(): lax.ppermute(x, 'tm', [(i, (i + by) % devices ^ mask) for i in range(devi...  10.5 us
    all_to_all x1, starting transfers between devices, body(): lax.all_to_all(regrouped(perambulator, high, half, pair_count, given_coun...  7.24 us
  transfers between devices with their start and end apart: 10, of which 6 were waited for; matrix products, arithmetic and copies ran while one was open for 1% of the time, Pallas kernels for 0%

profile of v1, /device:TPU:1, one launch (start us, length us, event | category | flops | bytes accessed | tf_op | source)
XLA Modules:
  0.0 298.7 jit_solution(15856945484110945567)
XLA Ops:
  0.0 0.0 copy-start
  0.0 0.8 slice_bitcast_fusion
  0.8 3.6 %collective-permute-start.1 = (s32[3]{0:T(128)S(1)}, s32[3]{0:T(128)S(1)}, u32[]{:S(2)}, u32[]{:S(2)}) collective-permute-start(s32[3]{0:T(128)S(1)} %get-tuple-element.6), channel_id=1, source_target_pairs={{0,5},{1,6},{2,7},{3,8},{4,9},{5,10},{6,11},{7,12},{8,13},{9,14},{... | collective-permute-start | bytes 44 | tf_op jit(solution)/shard_map/ppermute | solution.py:22
  4.5 0.5 collective-permute-start.2
  4.9 2.9 collective-permute-start
  7.8 1.1 collective-permute-done.refs_0_
  8.9 0.0 collective-permute-done.1.refs_1_
  8.9 0.0 collective-permute-done.2.refs_2_
  8.9 0.0 copy-start.7
  8.9 0.5 copy-done.12
  9.4 0.0 copy-done.9
  9.4 0.0 copy-done.7
  9.4 144.2 %shard_map.46 = bf16[8,2,2,48,1536]{4,3,2,1,0:T(8,128)(2,1)} custom-call(s32[1]{0:T(128)} %bitcast.high_ref, bf16[2,8,2,48,1536]{4,3,2,1,0:T(8,128)(2,1)} %bitcast.14, s32[2]{0:T(128)} %copy-done.12, s32[3]{0:T(128)} %copy-done.9, s32[3]{0:T(128)} %copy-done.7), custom_call_target="tpu_custom_call" | custom-call | tf_op jit(solution)/shard_map/pallas_call | solution.py:46
  153.6 0.0 copy-start.11
  153.6 0.0 copy-start.10
  153.6 7.2 %all-to-all-start = ((bf16[8,2,2,48,1536]{4,3,2,1,0:T(8,128)(2,1)}), bf16[8,2,2,48,1536]{4,3,2,1,0:T(8,128)(2,1)}, u32[]{:S(2)}, u32[]{:S(2)}) async-start(bf16[8,2,2,48,1536]{4,3,2,1,0:T(8,128)(2,1)} %shard_map.46), calls=%async_computation | async-start | bytes 9437184 | tf_op jit(solution)/shard_map/all_to_all | solution.py:186
  160.9 0.0 copy-done.11
  160.9 0.0 copy-start.14
  160.9 0.1 reshape.40
  161.0 0.0 copy-done
  161.0 0.7 gather_fusion.2
  161.8 0.1 collective-permute-start.7
  161.9 0.0 copy-done.10
  161.9 1.4 gather_fusion
  163.3 1.9 collective-permute-start.3
  165.2 0.0 copy-done.8
  165.2 1.4 gather_fusion.1
  166.6 3.0 collective-permute-start.4
  169.6 1.4 collective-permute-start.5
  171.0 0.0 collective-permute-start.6
  171.0 0.0 copy-done.13
  171.0 0.1 pad_add_fusion.counts_ref
  171.1 74.8 %collective-permute-done.3.refs_0_ = bf16[3,192,384]{2,1,0:T(8,128)(2,1)} collective-permute-done((bf16[3,192,384]{2,1,0:T(8,128)(2,1)}, bf16[3,192,384]{2,1,0:T(8,128)(2,1)}, u32[]{:S(2)}, u32[]{:S(2)}) %collective-permute-start.3) | collective-permute-done | bytes 442400 | tf_op jit(solution)/shard_map/ppermute | solution.py:22
  245.9 8.0 %collective-permute-done.4.refs_1_ = bf16[3,192,384]{2,1,0:T(8,128)(2,1)S(1)} collective-permute-done((bf16[3,192,384]{2,1,0:T(8,128)(2,1)}, bf16[3,192,384]{2,1,0:T(8,128)(2,1)S(1)}, u32[]{:S(2)}, u32[]{:S(2)}) %collective-permute-start.4) | collective-permute-done | bytes 442400 | tf_op jit(solution)/shard_map/ppermute | solution.py:22
  253.9 0.8 copy-done.1
  254.7 8.7 %collective-permute-done.5.refs_2_ = bf16[3,192,384]{2,1,0:T(8,128)(2,1)S(1)} collective-permute-done((bf16[3,192,384]{2,1,0:T(8,128)(2,1)}, bf16[3,192,384]{2,1,0:T(8,128)(2,1)S(1)}, u32[]{:S(2)}, u32[]{:S(2)}) %collective-permute-start.5) | collective-permute-done | bytes 442400 | tf_op jit(solution)/shard_map/ppermute | solution.py:22
  263.4 0.8 copy-done.3
  264.2 4.2 %collective-permute-done.6.refs_3_ = bf16[3,192,384]{2,1,0:T(8,128)(2,1)S(1)} collective-permute-done((bf16[3,192,384]{2,1,0:T(8,128)(2,1)}, bf16[3,192,384]{2,1,0:T(8,128)(2,1)S(1)}, u32[]{:S(2)}, u32[]{:S(2)}) %collective-permute-start.6) | collective-permute-done | bytes 442400 | tf_op jit(solution)/shard_map/ppermute | solution.py:22
  268.4 0.8 copy-done.5
  269.2 0.0 collective-permute-done.7.refs_4_
  269.2 0.0 all-to-all-done
  269.2 1.0 copy-done.2
  270.2 1.0 copy-done.4
  271.2 1.0 copy-done.6
  272.2 22.4 %shard_map.47 = f32[4,3,2]{2,1,0:T(4,128)S(1)} custom-call(s32[4]{0:T(128)S(1)} %pad_add_fusion.counts_ref, bf16[8,4,48,1536]{3,2,1,0:T(8,128)(2,1)} %bitcast.4.tau_ref, bf16[3,192,384]{2,1,0:T(8,128)(2,1)} %collective-permute-done.3.refs_0_, bf16[3,192,384]{2,1,0:T(8,128)(2,1)S(1)} %copy-done.2, bf16[3,192,384]{2,1,0:T(8,128)(2,1)S(1)} %copy-done.4, ...), custom_call_target="tpu_custom_call" | custom-call | flops 10871635968 | bytes 8257536 | tf_op jit(solution)/shard_map/pallas_call | solution.py:145
  294.6 0.1 collective-permute-start.8
  294.7 3.3 %collective-permute-done.8 = f32[2,3,2]{2,1,0:T(4,128)S(1)} collective-permute-done((f32[2,3,2]{2,1,0:T(4,128)S(1)}, f32[2,3,2]{2,1,0:T(4,128)S(1)}, u32[]{:S(2)}, u32[]{:S(2)}) %collective-permute-start.8) | collective-permute-done | bytes 80 | tf_op jit(solution)/shard_map/ppermute | solution.py:17
  298.0 0.7 copy.6
  (17 shorter events, 0.1 us)
Async XLA Ops:
  0.0 161.0 %copy-start = (bf16[1,16,192,384]{3,2,1,0:T(8,128)(2,1)S(1)}, bf16[1,16,192,384]{3,2,1,0:T(8,128)(2,1)}, u32[]{:S(2)}) copy-start(bf16[1,16,192,384]{3,2,1,0:T(8,128)(2,1)} %param.5) | copy-start | bytes 7077892
  0.8 8.0 %collective-permute-start.1 = (s32[3]{0:T(128)S(1)}, s32[3]{0:T(128)S(1)}, u32[]{:S(2)}, u32[]{:S(2)}) collective-permute-start(s32[3]{0:T(128)S(1)} %get-tuple-element.6), channel_id=1, source_target_pairs={{0,5},{1,6},{2,7},{3,8},{4,9},{5,10},{6,11},{7,12},{8,13},{9,14},{... | collective-permute-start | bytes 44 | tf_op jit(solution)/shard_map/ppermute | solution.py:22
  4.5 4.4 %collective-permute-start.2 = (s32[3]{0:T(128)S(1)}, s32[3]{0:T(128)S(1)}, u32[]{:S(2)}, u32[]{:S(2)}) collective-permute-start(s32[3]{0:T(128)S(1)} %get-tuple-element.5), channel_id=1, source_target_pairs={{0,10},{1,11},{2,12},{3,13},{4,14},{5,15},{6,0},{7,1},{8,2},{9,3},... | collective-permute-start | bytes 44 | tf_op jit(solution)/shard_map/ppermute | solution.py:22
  4.9 3.9 %collective-permute-start = (s32[2]{0:T(128)}, s32[2]{0:T(128)S(1)}, u32[]{:S(2)}, u32[]{:S(2)}) collective-permute-start(s32[2]{0:T(128)} %param.7), channel_id=1, source_target_pairs={{0,8},{1,9},{2,10},{3,11},{4,12},{5,13},{6,14},{7,15},{8,0},{9,1},... | collective-permute-start | bytes 32 | tf_op jit(solution)/shard_map/ppermute | solution.py:17
  8.9 0.5 copy-start.12
  8.9 0.5 copy-start.9
  8.9 0.5 copy-start.7
  153.6 7.3 %copy-start.11 = (s32[2,3,2]{1,2,0:T(2,128)S(1)}, s32[2,3,2]{1,2,0:T(2,128)}, u32[]{:S(2)}) copy-start(s32[2,3,2]{1,2,0:T(2,128)} %param.6) | copy-start | bytes 148
  153.6 8.3 %copy-start.10 = (s32[3]{0:T(128)S(1)}, s32[3]{0:T(128)}, u32[]{:S(2)}) copy-start(s32[3]{0:T(128)} %copy-done.9) | copy-start | bytes 40
  153.6 115.5 %all-to-all-start = ((bf16[8,2,2,48,1536]{4,3,2,1,0:T(8,128)(2,1)}), bf16[8,2,2,48,1536]{4,3,2,1,0:T(8,128)(2,1)}, u32[]{:S(2)}, u32[]{:S(2)}) async-start(bf16[8,2,2,48,1536]{4,3,2,1,0:T(8,128)(2,1)} %shard_map.46), calls=%async_computation | async-start | bytes 9437184 | tf_op jit(solution)/shard_map/all_to_all | solution.py:186
  160.9 4.3 %copy-start.8 = (s32[3]{0:T(128)S(1)}, s32[3]{0:T(128)}, u32[]{:S(2)}) copy-start(s32[3]{0:T(128)} %copy-done.7) | copy-start | bytes 40
  160.9 10.2 %copy-start.13 = (s32[2]{0:T(128)S(1)}, s32[2]{0:T(128)}, u32[]{:S(2)}) copy-start(s32[2]{0:T(128)} %copy-done.12) | copy-start | bytes 28
  160.9 10.1 %copy-start.14 = (s32[2]{0:T(128)S(1)}, s32[2]{0:T(128)}, u32[]{:S(2)}) copy-start(s32[2]{0:T(128)} %param.7) | copy-start | bytes 28
  161.8 107.4 %collective-permute-start.7 = (bf16[2,3,192,384]{3,2,1,0:T(8,128)(2,1)S(1)}, bf16[2,3,192,384]{3,2,1,0:T(8,128)(2,1)}, u32[]{:S(2)}, u32[]{:S(2)}) collective-permute-start(bf16[2,3,192,384]{3,2,1,0:T(8,128)(2,1)S(1)} %bitcast.12), channel_id=1, source_target_pairs={{0,8},{1,9},{2,10},{3,11},{4,12},{5,13},{6,14},{7,15},{8,0},{9,1},... | collective-permute-start | bytes 2654216 | tf_op jit(solution)/shard_map/ppermute | solution.py:17
  163.3 82.6 %collective-permute-start.3 = (bf16[3,192,384]{2,1,0:T(8,128)(2,1)}, bf16[3,192,384]{2,1,0:T(8,128)(2,1)}, u32[]{:S(2)}, u32[]{:S(2)}) collective-permute-start(bf16[3,192,384]{2,1,0:T(8,128)(2,1)} %gather_fusion), channel_id=1, source_target_pairs={{0,3},{1,4},{2,5},{3,6},{4,7},{5,8},{6,9},{7,10},{8,11},{9,12},{10... | collective-permute-start | bytes 1327112 | tf_op jit(solution)/shard_map/ppermute | solution.py:22
  166.6 87.3 %collective-permute-start.4 = (bf16[3,192,384]{2,1,0:T(8,128)(2,1)}, bf16[3,192,384]{2,1,0:T(8,128)(2,1)S(1)}, u32[]{:S(2)}, u32[]{:S(2)}) collective-permute-start(bf16[3,192,384]{2,1,0:T(8,128)(2,1)} %gather_fusion.1), channel_id=1, source_target_pairs={{0,14},{1,15},{2,0},{3,1},{4,2},{5,3},{6,4},{7,5},{8,6},{9,7},{10,... | collective-permute-start | bytes 1327112 | tf_op jit(solution)/shard_map/ppermute | solution.py:22
  169.6 93.8 %collective-permute-start.5 = (bf16[3,192,384]{2,1,0:T(8,128)(2,1)}, bf16[3,192,384]{2,1,0:T(8,128)(2,1)S(1)}, u32[]{:S(2)}, u32[]{:S(2)}) collective-permute-start(bf16[3,192,384]{2,1,0:T(8,128)(2,1)} %gather_fusion), channel_id=1, source_target_pairs={{0,11},{1,12},{2,13},{3,14},{4,15},{5,0},{6,1},{7,2},{8,3},{9,4},{... | collective-permute-start | bytes 1327112 | tf_op jit(solution)/shard_map/ppermute | solution.py:22
  171.0 97.4 %collective-permute-start.6 = (bf16[3,192,384]{2,1,0:T(8,128)(2,1)}, bf16[3,192,384]{2,1,0:T(8,128)(2,1)S(1)}, u32[]{:S(2)}, u32[]{:S(2)}) collective-permute-start(bf16[3,192,384]{2,1,0:T(8,128)(2,1)} %gather_fusion.1), channel_id=1, source_target_pairs={{0,6},{1,7},{2,8},{3,9},{4,10},{5,11},{6,12},{7,13},{8,14},{9,15},... | collective-permute-start | bytes 1327112 | tf_op jit(solution)/shard_map/ppermute | solution.py:22
  253.9 0.8 copy-start.1
  263.4 0.8 copy-start.3
  268.4 0.8 copy-start.5
  269.2 1.0 copy-start.2
  270.2 1.0 copy-start.4
  271.2 1.0 copy-start.6
  294.6 3.4 %collective-permute-start.8 = (f32[2,3,2]{2,1,0:T(4,128)S(1)}, f32[2,3,2]{2,1,0:T(4,128)S(1)}, u32[]{:S(2)}, u32[]{:S(2)}) collective-permute-start(f32[2,3,2]{2,1,0:T(4,128)S(1)} %slice.27), channel_id=1, source_target_pairs={{0,8},{1,9},{2,10},{3,11},{4,12},{5,13},{6,14},{7,15},{8,0},{9,1},... | collective-permute-start | bytes 152 | tf_op jit(solution)/shard_map/ppermute | solution.py:17

commit v2 on v1

--- a/solution.py
+++ b/solution.py
@@ -9,6 +9,7 @@
 
 NT_DIMS = (((1,), (1,)), ((), ()))
 ANYWHERE = pl.BlockSpec(memory_space=pl.ANY)
+HBM = pl.BlockSpec(memory_space=pltpu.HBM)
 SMEM = pl.BlockSpec(memory_space=pltpu.SMEM)
 
 
@@ -22,8 +23,7 @@
     return lax.ppermute(x, "tm", [(i, ((i + by) % devices) ^ mask) for i in range(devices)])
 
 
-def regroup_kernel(high_ref, source_ref, *refs):
-    out_ref, sems = refs[-2:]
+def regroup_kernel(high_ref, source_ref, out_ref, sems):
     high = high_ref[0]
     copies = []
     for j in range(source_ref.shape[1]):
@@ -40,16 +40,27 @@
         copy.wait()
 
 
-def regrouped(perambulator, high, half, pair_count, *earlier):
+def regrouped(perambulator, high, half, pair_count):
     columns, width = perambulator.shape[1:]
     source = perambulator.reshape(2, half, pair_count, columns, width)
     return pl.pallas_call(
         regroup_kernel,
-        in_specs=[SMEM, ANYWHERE] + [ANYWHERE] * len(earlier),
-        out_specs=ANYWHERE,
+        in_specs=[SMEM, HBM],
+        out_specs=pl.BlockSpec(memory_space=pltpu.VMEM),
         out_shape=jax.ShapeDtypeStruct((half, 2, pair_count, columns, width), perambulator.dtype),
         scratch_shapes=[pltpu.SemaphoreType.DMA((2 * half,))],
-    )(high.reshape(1), source, *earlier)
+        compiler_params=pltpu.CompilerParams(vmem_limit_bytes=56 * 1024 * 1024),
+    )(high.reshape(1), source)
+
+
+def tied(x, *earlier):
+    return pl.pallas_call(
+        lambda *refs: None,
+        in_specs=[ANYWHERE] * (1 + len(earlier)),
+        out_specs=ANYWHERE,
+        out_shape=jax.ShapeDtypeStruct(x.shape, x.dtype),
+        input_output_aliases={0: 0},
+    )(x, *earlier)
 
 
 def halves_swapped(x):
@@ -146,7 +157,7 @@
         functools.partial(pairs_kernel, pairs // 2),
         grid=(pairs,),
         in_specs=[SMEM, pl.BlockSpec((pieces, 1, columns, width), lambda p: (0, p, 0, 0))]
-        + [ANYWHERE] * (pairs + 2),
+        + [HBM] * (pairs + 2),
         out_specs=SMEM,
         out_shape=jax.ShapeDtypeStruct((pairs, slots, 2), jnp.float32),
         scratch_shapes=[
@@ -157,7 +168,7 @@
             pltpu.SemaphoreType.DMA((pairs, slots)),
             pltpu.SemaphoreType.DMA((pairs, slots)),
         ],
-        compiler_params=pltpu.CompilerParams(vmem_limit_bytes=40 * 1024 * 1024),
+        compiler_params=pltpu.CompilerParams(vmem_limit_bytes=56 * 1024 * 1024),
         cost_estimate=pl.CostEstimate(flops=flops, bytes_accessed=moved, transcendentals=0),
     )(counts, tau, *sinks, *sources)
 
@@ -184,7 +195,7 @@
     own_sinks = [passed_along(sets, -by) for by, sets in zip(steps, chosen)]
 
     tau = lax.all_to_all(
-        regrouped(perambulator, high, half, pair_count, given_counts, *wanted),
+        tied(regrouped(perambulator, high, half, pair_count), given_counts, *wanted),
         "tm",
         split_axis=0,
         concat_axis=0,

time: 297 us -> 152 us (0.51)
  the two profiles are of different devices: /device:TPU:1 before, /device:TPU:5 now
where the time goes in v2:
time: 152 us; the launch traced here: 154 us
  waiting for transfers between devices  98.6 us (65%)
  Pallas kernels  29 us (19%)
  starting transfers between devices  18 us (12%)
  local copies, waits for them, and re-layouts  6.94 us (5%)
    ppermute x6, waiting for transfers between devices, passed_along(): lax.ppermute(x, 'tm', [(i, (i + by) % devices ^ mask) for i in range(devi...  95.3 us
    pallas_call x1, Pallas kernels, pairs_sums(): pl.pallas_call(functools.partial(pairs_kernel, pairs // 2), grid=(pairs,)...  24.4 us
    ppermute x6, starting transfers between devices, passed_along(): lax.ppermute(x, 'tm', [(i, (i + by) % devices ^ mask) for i in range(devi...  10 us
    all_to_all x1, starting transfers between devices, body(): lax.all_to_all(tied(regrouped(perambulator, high, half, pair_count), give...  5.11 us
    pallas_call x1, Pallas kernels, regrouped(): pl.pallas_call(regroup_kernel, in_specs=[SMEM, HBM], out_specs=pl.BlockSp...  4.61 us
    ppermute x3, waiting for transfers between devices, exchanged(): return lax.ppermute(x, 'tm', [(i, i ^ mask) for i in range(devices)])  3.36 us
  transfers between devices with their start and end apart: 10, of which 4 were waited for; matrix products, arithmetic and copies ran while one was open for 3% of the time, Pallas kernels for 3%

profile of v2, /device:TPU:5, one launch (start us, length us, event | category | flops | bytes accessed | tf_op | source)
XLA Modules:
  0.0 154.0 jit_solution(12501230328531931742)
XLA Ops:
  0.0 0.0 copy-start
  0.0 0.8 slice_bitcast_fusion
  0.8 2.8 %collective-permute-start.1 = (s32[3]{0:T(128)S(1)}, s32[3]{0:T(128)S(1)}, u32[]{:S(2)}, u32[]{:S(2)}) collective-permute-start(s32[3]{0:T(128)S(1)} %get-tuple-element.6), channel_id=1, source_target_pairs={{0,5},{1,6},{2,7},{3,8},{4,9},{5,10},{6,11},{7,12},{8,13},{9,14},{... | collective-permute-start | bytes 44 | tf_op jit(solution)/shard_map/ppermute | solution.py:23
  3.7 1.9 %collective-permute-start.2 = (s32[3]{0:T(128)S(1)}, s32[3]{0:T(128)S(1)}, u32[]{:S(2)}, u32[]{:S(2)}) collective-permute-start(s32[3]{0:T(128)S(1)} %get-tuple-element.5), channel_id=1, source_target_pairs={{0,10},{1,11},{2,12},{3,13},{4,14},{5,15},{6,0},{7,1},{8,2},{9,3},... | collective-permute-start | bytes 44 | tf_op jit(solution)/shard_map/ppermute | solution.py:23
  5.6 0.5 collective-permute-start
  6.1 4.6 %shard_map.46.refs_0_ = bf16[8,2,2,48,1536]{4,3,2,1,0:T(8,128)(2,1)} custom-call(s32[1]{0:T(128)} %bitcast.high_ref, bf16[2,8,2,48,1536]{4,3,2,1,0:T(8,128)(2,1)} %bitcast.12), custom_call_target="tpu_custom_call" | custom-call | tf_op jit(solution)/shard_map/pallas_call | solution.py:46
  10.7 0.0 collective-permute-done.refs_1_
  10.7 0.0 copy-start.7
  10.7 0.0 collective-permute-done.1.refs_2_
  10.7 0.0 copy-start.4
  10.7 0.0 collective-permute-done.2.refs_3_
  10.8 0.5 copy-done.7
  11.2 0.1 copy-done.4
  11.3 0.0 copy-start.2
  11.3 0.6 copy-done.2
  11.9 0.0 copy-start.6
  11.9 0.0 copy-start.9
  11.9 5.1 %all-to-all-start = ((bf16[8,2,2,48,1536]{4,3,2,1,0:T(8,128)(2,1)}), bf16[8,2,2,48,1536]{4,3,2,1,0:T(8,128)(2,1)}, u32[]{:S(2)}, u32[]{:S(2)}) async-start(bf16[8,2,2,48,1536]{4,3,2,1,0:T(8,128)(2,1)} %shard_map.47), calls=%async_computation | async-start | bytes 9437184 | tf_op jit(solution)/shard_map/all_to_all | solution.py:197
  17.0 0.0 copy-done.6
  17.0 0.1 reshape.40
  17.1 0.0 copy-done
  17.1 0.7 gather_fusion.2
  17.9 0.0 copy-start.1
  17.9 2.4 %collective-permute-start.7 = (bf16[2,3,192,384]{3,2,1,0:T(8,128)(2,1)S(1)}, bf16[2,3,192,384]{3,2,1,0:T(8,128)(2,1)}, u32[]{:S(2)}, u32[]{:S(2)}) collective-permute-start(bf16[2,3,192,384]{3,2,1,0:T(8,128)(2,1)S(1)} %bitcast.13), channel_id=1, source_target_pairs={{0,8},{1,9},{2,10},{3,11},{4,12},{5,13},{6,14},{7,15},{8,0},{9,1},... | collective-permute-start | bytes 2654216 | tf_op jit(solution)/shard_map/ppermute | solution.py:18
  20.2 0.0 copy-done.5
  20.3 1.4 gather_fusion
  21.7 1.7 %collective-permute-start.3 = (bf16[3,192,384]{2,1,0:T(8,128)(2,1)}, bf16[3,192,384]{2,1,0:T(8,128)(2,1)}, u32[]{:S(2)}, u32[]{:S(2)}) collective-permute-start(bf16[3,192,384]{2,1,0:T(8,128)(2,1)} %gather_fusion), channel_id=1, source_target_pairs={{0,3},{1,4},{2,5},{3,6},{4,7},{5,8},{6,9},{7,10},{8,11},{9,12},{10... | collective-permute-start | bytes 1327112 | tf_op jit(solution)/shard_map/ppermute | solution.py:23
  23.4 0.0 copy-done.3
  23.4 1.4 gather_fusion.1
  24.8 0.3 collective-permute-start.4
  25.0 1.3 collective-permute-start.5
  26.4 2.0 %collective-permute-start.6 = (bf16[3,192,384]{2,1,0:T(8,128)(2,1)}, bf16[3,192,384]{2,1,0:T(8,128)(2,1)}, u32[]{:S(2)}, u32[]{:S(2)}) collective-permute-start(bf16[3,192,384]{2,1,0:T(8,128)(2,1)} %gather_fusion.1), channel_id=1, source_target_pairs={{0,6},{1,7},{2,8},{3,9},{4,10},{5,11},{6,12},{7,13},{8,14},{9,15},... | collective-permute-start | bytes 1327112 | tf_op jit(solution)/shard_map/ppermute | solution.py:23
  28.3 0.0 copy-done.8
  28.3 0.0 copy-done.9
  28.3 0.6 pad_add_fusion.counts_ref
  28.9 69.6 %collective-permute-done.3.refs_0_ = bf16[3,192,384]{2,1,0:T(8,128)(2,1)} collective-permute-done((bf16[3,192,384]{2,1,0:T(8,128)(2,1)}, bf16[3,192,384]{2,1,0:T(8,128)(2,1)}, u32[]{:S(2)}, u32[]{:S(2)}) %collective-permute-start.3) | collective-permute-done | bytes 442400 | tf_op jit(solution)/shard_map/ppermute | solution.py:23
  98.6 10.1 %collective-permute-done.4.refs_1_ = bf16[3,192,384]{2,1,0:T(8,128)(2,1)} collective-permute-done((bf16[3,192,384]{2,1,0:T(8,128)(2,1)}, bf16[3,192,384]{2,1,0:T(8,128)(2,1)}, u32[]{:S(2)}, u32[]{:S(2)}) %collective-permute-start.4) | collective-permute-done | bytes 442400 | tf_op jit(solution)/shard_map/ppermute | solution.py:23
  108.7 0.0 collective-permute-done.5.refs_2_
  108.7 15.5 %collective-permute-done.6.refs_3_ = bf16[3,192,384]{2,1,0:T(8,128)(2,1)} collective-permute-done((bf16[3,192,384]{2,1,0:T(8,128)(2,1)}, bf16[3,192,384]{2,1,0:T(8,128)(2,1)}, u32[]{:S(2)}, u32[]{:S(2)}) %collective-permute-start.6) | collective-permute-done | bytes 442400 | tf_op jit(solution)/shard_map/ppermute | solution.py:23
  124.2 0.0 collective-permute-done.7.refs_4_
  124.2 0.0 all-to-all-done
  124.2 0.0 copy-done.1
  124.2 24.4 %shard_map.48 = f32[4,3,2]{2,1,0:T(4,128)} custom-call(s32[4]{0:T(128)} %pad_add_fusion.counts_ref, bf16[8,4,48,1536]{3,2,1,0:T(8,128)(2,1)} %bitcast.4.tau_ref, bf16[3,192,384]{2,1,0:T(8,128)(2,1)} %collective-permute-done.3.refs_0_, bf16[3,192,384]{2,1,0:T(8,128)(2,1)} %collective-permute-done.4.refs_1_, ...), custom_call_target="tpu_custom_call" | custom-call | flops 10871635968 | bytes 8257536 | tf_op jit(solution)/shard_map/pallas_call | solution.py:156
  148.6 0.7 slice.27
  149.3 0.0 collective-permute-start.8
  149.3 3.4 %collective-permute-done.8 = f32[2,3,2]{2,1,0:T(4,128)S(1)} collective-permute-done((f32[2,3,2]{2,1,0:T(4,128)S(1)}, f32[2,3,2]{2,1,0:T(4,128)S(1)}, u32[]{:S(2)}, u32[]{:S(2)}) %collective-permute-start.8) | collective-permute-done | bytes 80 | tf_op jit(solution)/shard_map/ppermute | solution.py:18
  152.6 0.7 fusion
  153.3 0.7 copy.7
  (8 shorter events, 0.0 us)
Async XLA Ops:
  0.0 17.1 %copy-start = (bf16[1,16,192,384]{3,2,1,0:T(8,128)(2,1)S(1)}, bf16[1,16,192,384]{3,2,1,0:T(8,128)(2,1)}, u32[]{:S(2)}) copy-start(bf16[1,16,192,384]{3,2,1,0:T(8,128)(2,1)} %param.5) | copy-start | bytes 7077892
  0.8 9.9 %collective-permute-start.1 = (s32[3]{0:T(128)S(1)}, s32[3]{0:T(128)S(1)}, u32[]{:S(2)}, u32[]{:S(2)}) collective-permute-start(s32[3]{0:T(128)S(1)} %get-tuple-element.6), channel_id=1, source_target_pairs={{0,5},{1,6},{2,7},{3,8},{4,9},{5,10},{6,11},{7,12},{8,13},{9,14},{... | collective-permute-start | bytes 44 | tf_op jit(solution)/shard_map/ppermute | solution.py:23
  3.7 7.1 %collective-permute-start.2 = (s32[3]{0:T(128)S(1)}, s32[3]{0:T(128)S(1)}, u32[]{:S(2)}, u32[]{:S(2)}) collective-permute-start(s32[3]{0:T(128)S(1)} %get-tuple-element.5), channel_id=1, source_target_pairs={{0,10},{1,11},{2,12},{3,13},{4,14},{5,15},{6,0},{7,1},{8,2},{9,3},... | collective-permute-start | bytes 44 | tf_op jit(solution)/shard_map/ppermute | solution.py:23
  5.6 5.1 %collective-permute-start = (s32[2]{0:T(128)}, s32[2]{0:T(128)S(1)}, u32[]{:S(2)}, u32[]{:S(2)}) collective-permute-start(s32[2]{0:T(128)} %param.7), channel_id=1, source_target_pairs={{0,8},{1,9},{2,10},{3,11},{4,12},{5,13},{6,14},{7,15},{8,0},{9,1},... | collective-permute-start | bytes 32 | tf_op jit(solution)/shard_map/ppermute | solution.py:18
  10.7 0.5 copy-start.7
  10.7 0.5 copy-start.4
  11.3 0.6 copy-start.2
  11.9 5.1 %copy-start.6 = (s32[2,3,2]{1,2,0:T(2,128)S(1)}, s32[2,3,2]{1,2,0:T(2,128)}, u32[]{:S(2)}) copy-start(s32[2,3,2]{1,2,0:T(2,128)} %param.6) | copy-start | bytes 148
  11.9 8.4 %copy-start.5 = (s32[3]{0:T(128)S(1)}, s32[3]{0:T(128)}, u32[]{:S(2)}) copy-start(s32[3]{0:T(128)} %copy-done.4) | copy-start | bytes 40
  11.9 11.5 %copy-start.3 = (s32[3]{0:T(128)S(1)}, s32[3]{0:T(128)}, u32[]{:S(2)}) copy-start(s32[3]{0:T(128)} %copy-done.2) | copy-start | bytes 40
  11.9 16.5 %copy-start.8 = (s32[2]{0:T(128)S(1)}, s32[2]{0:T(128)}, u32[]{:S(2)}) copy-start(s32[2]{0:T(128)} %copy-done.7) | copy-start | bytes 28
  11.9 16.5 %copy-start.9 = (s32[2]{0:T(128)S(1)}, s32[2]{0:T(128)}, u32[]{:S(2)}) copy-start(s32[2]{0:T(128)} %param.7) | copy-start | bytes 28
  11.9 112.3 %all-to-all-start = ((bf16[8,2,2,48,1536]{4,3,2,1,0:T(8,128)(2,1)}), bf16[8,2,2,48,1536]{4,3,2,1,0:T(8,128)(2,1)}, u32[]{:S(2)}, u32[]{:S(2)}) async-start(bf16[8,2,2,48,1536]{4,3,2,1,0:T(8,128)(2,1)} %shard_map.47), calls=%async_computation | async-start | bytes 9437184 | tf_op jit(solution)/shard_map/all_to_all | solution.py:197
  17.9 106.3 %copy-start.1 = (bf16[6,192,384]{2,1,0:T(8,128)(2,1)}, bf16[6,192,384]{2,1,0:T(8,128)(2,1)S(1)}, u32[]{:S(2)}) copy-start(bf16[6,192,384]{2,1,0:T(8,128)(2,1)S(1)} %gather_fusion.2) | copy-start | bytes 2654212
  17.9 106.3 %collective-permute-start.7 = (bf16[2,3,192,384]{3,2,1,0:T(8,128)(2,1)S(1)}, bf16[2,3,192,384]{3,2,1,0:T(8,128)(2,1)}, u32[]{:S(2)}, u32[]{:S(2)}) collective-permute-start(bf16[2,3,192,384]{3,2,1,0:T(8,128)(2,1)S(1)} %bitcast.13), channel_id=1, source_target_pairs={{0,8},{1,9},{2,10},{3,11},{4,12},{5,13},{6,14},{7,15},{8,0},{9,1},... | collective-permute-start | bytes 2654216 | tf_op jit(solution)/shard_map/ppermute | solution.py:18
  21.7 76.9 %collective-permute-start.3 = (bf16[3,192,384]{2,1,0:T(8,128)(2,1)}, bf16[3,192,384]{2,1,0:T(8,128)(2,1)}, u32[]{:S(2)}, u32[]{:S(2)}) collective-permute-start(bf16[3,192,384]{2,1,0:T(8,128)(2,1)} %gather_fusion), channel_id=1, source_target_pairs={{0,3},{1,4},{2,5},{3,6},{4,7},{5,8},{6,9},{7,10},{8,11},{9,12},{10... | collective-permute-start | bytes 1327112 | tf_op jit(solution)/shard_map/ppermute | solution.py:23
  24.8 83.9 %collective-permute-start.4 = (bf16[3,192,384]{2,1,0:T(8,128)(2,1)}, bf16[3,192,384]{2,1,0:T(8,128)(2,1)}, u32[]{:S(2)}, u32[]{:S(2)}) collective-permute-start(bf16[3,192,384]{2,1,0:T(8,128)(2,1)} %gather_fusion.1), channel_id=1, source_target_pairs={{0,14},{1,15},{2,0},{3,1},{4,2},{5,3},{6,4},{7,5},{8,6},{9,7},{10,... | collective-permute-start | bytes 1327112 | tf_op jit(solution)/shard_map/ppermute | solution.py:23
  25.0 83.7 %collective-permute-start.5 = (bf16[3,192,384]{2,1,0:T(8,128)(2,1)}, bf16[3,192,384]{2,1,0:T(8,128)(2,1)}, u32[]{:S(2)}, u32[]{:S(2)}) collective-permute-start(bf16[3,192,384]{2,1,0:T(8,128)(2,1)} %gather_fusion), channel_id=1, source_target_pairs={{0,11},{1,12},{2,13},{3,14},{4,15},{5,0},{6,1},{7,2},{8,3},{9,4},{... | collective-permute-start | bytes 1327112 | tf_op jit(solution)/shard_map/ppermute | solution.py:23
  26.4 97.8 %collective-permute-start.6 = (bf16[3,192,384]{2,1,0:T(8,128)(2,1)}, bf16[3,192,384]{2,1,0:T(8,128)(2,1)}, u32[]{:S(2)}, u32[]{:S(2)}) collective-permute-start(bf16[3,192,384]{2,1,0:T(8,128)(2,1)} %gather_fusion.1), channel_id=1, source_target_pairs={{0,6},{1,7},{2,8},{3,9},{4,10},{5,11},{6,12},{7,13},{8,14},{9,15},... | collective-permute-start | bytes 1327112 | tf_op jit(solution)/shard_map/ppermute | solution.py:23
  149.3 3.4 %collective-permute-start.8 = (f32[2,3,2]{2,1,0:T(4,128)S(1)}, f32[2,3,2]{2,1,0:T(4,128)S(1)}, u32[]{:S(2)}, u32[]{:S(2)}) collective-permute-start(f32[2,3,2]{2,1,0:T(4,128)S(1)} %slice.27), channel_id=1, source_target_pairs={{0,8},{1,9},{2,10},{3,11},{4,12},{5,13},{6,14},{7,15},{8,0},{9,1},... | collective-permute-start | bytes 152 | tf_op jit(solution)/shard_map/ppermute | solution.py:18

commit v3 on v2

--- a/solution.py
+++ b/solution.py
@@ -23,34 +23,26 @@
     return lax.ppermute(x, "tm", [(i, ((i + by) % devices) ^ mask) for i in range(devices)])
 
 
-def regroup_kernel(high_ref, source_ref, out_ref, sems):
-    high = high_ref[0]
-    copies = []
-    for j in range(source_ref.shape[1]):
-        for side in range(2):
-            which = 1 - high if side == 0 else high
-            copies.append(
-                pltpu.make_async_copy(
-                    source_ref.at[which, j], out_ref.at[j, side], sems.at[2 * j + side]
-                )
-            )
+def slice_kernel(which_ref, source_ref, out_ref, sems):
+    copies = [
+        pltpu.make_async_copy(source_ref.at[which_ref[0], j], out_ref.at[j], sems.at[j])
+        for j in range(source_ref.shape[1])
+    ]
     for copy in copies:
         copy.start()
     for copy in copies:
         copy.wait()
 
 
-def regrouped(perambulator, high, half, pair_count):
-    columns, width = perambulator.shape[1:]
-    source = perambulator.reshape(2, half, pair_count, columns, width)
+def sliced(source, which):
     return pl.pallas_call(
-        regroup_kernel,
+        slice_kernel,
         in_specs=[SMEM, HBM],
         out_specs=pl.BlockSpec(memory_space=pltpu.VMEM),
-        out_shape=jax.ShapeDtypeStruct((half, 2, pair_count, columns, width), perambulator.dtype),
-        scratch_shapes=[pltpu.SemaphoreType.DMA((2 * half,))],
+        out_shape=jax.ShapeDtypeStruct(source.shape[1:], source.dtype),
+        scratch_shapes=[pltpu.SemaphoreType.DMA((source.shape[1],))],
         compiler_params=pltpu.CompilerParams(vmem_limit_bytes=56 * 1024 * 1024),
-    )(high.reshape(1), source)
+    )(which.reshape(1), source)
 
 
 def tied(x, *earlier):
@@ -68,9 +60,9 @@
     return jnp.concatenate([x[:, vectors:], x[:, :vectors]], axis=1)
 
 
-def pairs_kernel(pair_count, counts_ref, tau_ref, *refs):
-    sink_refs = refs[: 2 * pair_count]
-    source_refs = refs[2 * pair_count : 2 * pair_count + 2]
+def pairs_kernel(pairs, counts_ref, tau_ref, *refs):
+    sink_refs = refs[:pairs]
+    source_ref = refs[pairs]
     out_ref, sinks, sources, swap_ref, left_ref, sink_sems, source_sems = refs[-7:]
     slots, vectors, packed = sinks.shape[1:]
     spins, _, width = swap_ref.shape
@@ -81,8 +73,7 @@
 
     @pl.when(pair == 0)
     def _():
-        for p in range(2 * pair_count):
-            side, slot = divmod(p, pair_count)
+        for p in range(pairs):
             for d in range(slots):
                 out_ref[p, d, 0] = 0.0
                 out_ref[p, d, 1] = 0.0
@@ -93,7 +84,7 @@
                         sink_refs[p].at[d], sinks.at[p, d], sink_sems.at[p, d]
                     ).start()
                     pltpu.make_async_copy(
-                        source_refs[side].at[slot, d], sources.at[p, d], source_sems.at[p, d]
+                        source_ref.at[p, d], sources.at[p, d], source_sems.at[p, d]
                     ).start()
 
     def tile(s):
@@ -137,7 +128,7 @@
                 left_ref[s], swap_ref[s], NT_DIMS, preferred_element_type=jnp.float32
             )
         pltpu.make_async_copy(
-            source_refs[0].at[0, 0], sources.at[pair, d], source_sems.at[pair, d]
+            source_ref.at[0, 0], sources.at[pair, d], source_sems.at[pair, d]
         ).wait()
         source = sources[pair, d].astype(jnp.float32)
         real = source[:, :vectors]
@@ -146,7 +137,7 @@
         out_ref[pair, d, 1] = jnp.sum(real * block_imag + imag * block_real)
 
 
-def pairs_sums(tau, sinks, sources, counts):
+def pairs_sums(tau, sinks, sources, counts, *earlier):
     pairs = len(sinks)
     slots, vectors, packed = sinks[0].shape
     pieces, _, columns, width = tau.shape
@@ -154,10 +145,11 @@
     flops = 4 * pairs * spins * slots * width * vectors * packed
     moved = 2 * pairs * (spins * vectors * width + 2 * slots * vectors * packed)
     return pl.pallas_call(
-        functools.partial(pairs_kernel, pairs // 2),
+        functools.partial(pairs_kernel, pairs),
         grid=(pairs,),
         in_specs=[SMEM, pl.BlockSpec((pieces, 1, columns, width), lambda p: (0, p, 0, 0))]
-        + [HBM] * (pairs + 2),
+        + [HBM] * (pairs + 1)
+        + [ANYWHERE] * len(earlier),
         out_specs=SMEM,
         out_shape=jax.ShapeDtypeStruct((pairs, slots, 2), jnp.float32),
         scratch_shapes=[
@@ -170,7 +162,7 @@
         ],
         compiler_params=pltpu.CompilerParams(vmem_limit_bytes=56 * 1024 * 1024),
         cost_estimate=pl.CostEstimate(flops=flops, bytes_accessed=moved, transcendentals=0),
-    )(counts, tau, *sinks, *sources)
+    )(counts, tau, *sinks, sources, *earlier)
 
 
 def body(perambulator, elementals, diagrams, counts):
@@ -194,26 +186,28 @@
     given_sinks = [passed_along(sets, -by, half) for by, sets in zip(steps, chosen)]
     own_sinks = [passed_along(sets, -by) for by, sets in zip(steps, chosen)]
 
-    tau = lax.all_to_all(
-        tied(regrouped(perambulator, high, half, pair_count), given_counts, *wanted),
-        "tm",
-        split_axis=0,
-        concat_axis=0,
-        axis_index_groups=halves,
-        tiled=True,
-    ).reshape(half, 2 * pair_count, columns, width)
-    if columns % 16 != 0:
-        tau = jnp.moveaxis(tau, 1, 0).reshape(2 * pair_count, -1, vectors, width)
-        tau = jnp.moveaxis(tau, 0, 1)
-
-    sums = pairs_sums(
-        tau,
-        given_sinks + own_sinks,
-        (given_sources, own_sources),
-        jnp.concatenate([given_counts, counts]),
-    )
-    got = exchanged(sums[:pair_count], half)
-    return (sums[pair_count:] + got) / (columns * devices)
+    grouped = perambulator.reshape(2, half, pair_count, columns, width)
+
+    def regrouped(which, *earlier):
+        tau = lax.all_to_all(
+            tied(sliced(grouped, which), *earlier),
+            "tm",
+            split_axis=0,
+            concat_axis=0,
+            axis_index_groups=halves,
+            tiled=True,
+        )
+        if columns % 16 != 0:
+            tau = jnp.moveaxis(tau, 1, 0).reshape(pair_count, -1, vectors, width)
+            tau = jnp.moveaxis(tau, 0, 1)
+        return tau
+
+    given_tau = regrouped(1 - high, given_counts, *wanted)
+    own_tau = regrouped(high, given_tau, given_sources, *given_sinks)
+    given = pairs_sums(given_tau, given_sinks, given_sources, given_counts)
+    got = exchanged(given, half)
+    kept = pairs_sums(own_tau, own_sinks, own_sources, counts, given)
+    return (kept + got) / (columns * devices)
 
 
 def solution(mesh):

time: 152 us -> 148 us (0.974)
  the two profiles are of different devices: /device:TPU:5 before, /device:TPU:0 now
where the time goes in v3:
time: 148 us; the launch traced here: 150 us
  waiting for transfers between devices  77.3 us (52%)
  Pallas kernels  32.9 us (22%)
  starting transfers between devices  28.4 us (19%)
  local copies, waits for them, and re-layouts  10.4 us (7%)
    ppermute x6, waiting for transfers between devices, passed_along(): lax.ppermute(x, 'tm', [(i, (i + by) % devices ^ mask) for i in range(devi...  76.1 us
    pallas_call x2, Pallas kernels, pairs_sums(): pl.pallas_call(functools.partial(pairs_kernel, pairs), grid=(pairs,), in_...  26.8 us
    ppermute x6, starting transfers between devices, passed_along(): lax.ppermute(x, 'tm', [(i, (i + by) % devices ^ mask) for i in range(devi...  12.9 us
    all_to_all x2, starting transfers between devices, regrouped(): lax.all_to_all(tied(sliced(grouped, which), *earlier), 'tm', split_axis=0...  9.01 us
    ppermute x3, starting transfers between devices, exchanged(): return lax.ppermute(x, 'tm', [(i, i ^ mask) for i in range(devices)])  6.42 us
    pallas_call x2, Pallas kernels, sliced(): pl.pallas_call(slice_kernel, in_specs=[SMEM, HBM], out_specs=pl.BlockSpec...  6.16 us
    unnamed x26, local copies, waits for them, and re-layouts  4.39 us
  transfers between devices with their start and end apart: 11, of which 5 were waited for; matrix products, arithmetic and copies ran while one was open for 3% of the time, Pallas kernels for 22%

profile of v3, /device:TPU:0, one launch (start us, length us, event | category | flops | bytes accessed | tf_op | source)
XLA Modules:
  0.0 149.8 jit_solution(6751850278255632353)
XLA Ops:
  0.0 0.0 copy-start
  0.0 0.8 slice_bitcast_fusion
  0.8 5.0 %collective-permute-start.2 = (s32[3]{0:T(128)S(1)}, s32[3]{0:T(128)S(1)}, u32[]{:S(2)}, u32[]{:S(2)}) collective-permute-start(s32[3]{0:T(128)S(1)} %get-tuple-element.5), channel_id=1, source_target_pairs={{0,10},{1,11},{2,12},{3,13},{4,14},{5,15},{6,0},{7,1},{8,2},{9,3},... | collective-permute-start | bytes 44 | tf_op jit(solution)/shard_map/ppermute | solution.py:23
  5.8 0.7 collective-permute-start.1
  6.6 0.3 collective-permute-start
  6.9 3.1 %shard_map.47.refs_0_ = bf16[8,2,48,1536]{3,2,1,0:T(8,128)(2,1)} custom-call(s32[1]{0:T(128)} %bitcast.2.which_ref, bf16[2,8,2,48,1536]{4,3,2,1,0:T(8,128)(2,1)} %bitcast.12), custom_call_target="tpu_custom_call" | custom-call | tf_op jit(solution)/shard_map/pallas_call | solution.py:38
  10.0 1.1 collective-permute-done.refs_1_.counts_ref
  11.2 0.0 collective-permute-done.2.refs_3_
  11.2 0.0 collective-permute-done.1.refs_2_
  11.2 0.5 copy-done.11
  11.7 0.0 copy-done.7
  11.7 0.5 copy-done.9
  12.2 4.5 %all-to-all-start = ((bf16[8,2,48,1536]{3,2,1,0:T(8,128)(2,1)}), bf16[8,2,48,1536]{3,2,1,0:T(8,128)(2,1)}, u32[]{:S(2)}, u32[]{:S(2)}) async-start(bf16[8,2,48,1536]{3,2,1,0:T(8,128)(2,1)} %shard_map.48), calls=%async_computation | async-start | bytes 4718592 | tf_op jit(solution)/shard_map/all_to_all | solution.py:192
  16.7 0.0 copy-done.6
  16.7 0.0 copy-start.8
  16.7 0.1 reshape.19
  16.8 0.0 copy-done
  16.8 1.6 %gather_fusion = bf16[6,192,384]{2,1,0:T(8,128)(2,1)} fusion(bf16[16,192,384]{2,1,0:T(8,128)(2,1)S(1)} %bitcast.9, s32[1024]{0:T(1024)S(1)} %pad_clamp_fusion.2), kind=kCustom, calls=%fused_computation | custom fusion | bytes 1769496 | tf_op jit(solution)/shard_map/jit(_take)/gather | solution.py:182
  18.5 1.5 collective-permute-start.3
  19.9 0.0 copy-done.10
  19.9 1.4 gather_fusion.1
  21.3 0.0 copy-done.8
  21.3 1.4 gather_fusion.2
  22.8 3.7 %collective-permute-start.5 = (bf16[3,192,384]{2,1,0:T(8,128)(2,1)}, bf16[3,192,384]{2,1,0:T(8,128)(2,1)S(1)}, u32[]{:S(2)}, u32[]{:S(2)}) collective-permute-start(bf16[3,192,384]{2,1,0:T(8,128)(2,1)} %gather_fusion.2), channel_id=1, source_target_pairs={{0,14},{1,15},{2,0},{3,1},{4,2},{5,3},{6,4},{7,5},{8,6},{9,7},{10,... | collective-permute-start | bytes 1327112 | tf_op jit(solution)/shard_map/ppermute | solution.py:23
  26.4 0.0 collective-permute-start.4
  26.5 3.1 %shard_map.46.refs_0_ = bf16[8,2,48,1536]{3,2,1,0:T(8,128)(2,1)} custom-call(s32[1]{0:T(128)} %bitcast.which_ref, bf16[2,8,2,48,1536]{4,3,2,1,0:T(8,128)(2,1)} %bitcast.13), custom_call_target="tpu_custom_call" | custom-call | tf_op jit(solution)/shard_map/pallas_call | solution.py:38
  29.5 42.3 %collective-permute-done.5.refs_4_.refs_1_ = bf16[3,192,384]{2,1,0:T(8,128)(2,1)S(1)} collective-permute-done((bf16[3,192,384]{2,1,0:T(8,128)(2,1)}, bf16[3,192,384]{2,1,0:T(8,128)(2,1)S(1)}, u32[]{:S(2)}, u32[]{:S(2)}) %collective-permute-start.5) | collective-permute-done | bytes 442400 | tf_op jit(solution)/shard_map/ppermute | solution.py:23
  71.9 0.8 copy-done.4
  72.6 6.6 %collective-permute-done.4.refs_3_.refs_0_ = bf16[3,192,384]{2,1,0:T(8,128)(2,1)S(1)} collective-permute-done((bf16[3,192,384]{2,1,0:T(8,128)(2,1)}, bf16[3,192,384]{2,1,0:T(8,128)(2,1)S(1)}, u32[]{:S(2)}, u32[]{:S(2)}) %collective-permute-start.4) | collective-permute-done | bytes 442400 | tf_op jit(solution)/shard_map/ppermute | solution.py:23
  79.2 0.8 copy-done.5
  80.0 0.0 collective-permute-done.3.refs_2_
  80.0 0.0 all-to-all-done.refs_1_.tau_ref
  80.0 1.0 copy-done.1
  81.0 4.5 %all-to-all-start.1 = ((bf16[8,2,48,1536]{3,2,1,0:T(8,128)(2,1)}), bf16[8,2,48,1536]{3,2,1,0:T(8,128)(2,1)}, u32[]{:S(2)}, u32[]{:S(2)}) async-start(bf16[8,2,48,1536]{3,2,1,0:T(8,128)(2,1)} %shard_map.49), calls=%async_computation.1 | async-start | bytes 4718592 | tf_op jit(solution)/shard_map/all_to_all | solution.py:192
  85.5 0.0 copy-done.3
  85.5 2.8 %collective-permute-start.7 = (bf16[3,192,384]{2,1,0:T(8,128)(2,1)S(1)}, bf16[3,192,384]{2,1,0:T(8,128)(2,1)S(1)}, u32[]{:S(2)}, u32[]{:S(2)}) collective-permute-start(bf16[3,192,384]{2,1,0:T(8,128)(2,1)S(1)} %copy-done.3), channel_id=1, source_target_pairs={{0,6},{1,7},{2,8},{3,9},{4,10},{5,11},{6,12},{7,13},{8,14},{9,15},... | collective-permute-start | bytes 1327112 | tf_op jit(solution)/shard_map/ppermute | solution.py:23
  88.3 0.0 copy-done.2
  88.3 0.7 collective-permute-start.6
  89.0 11.4 %shard_map.50.refs_3_ = f32[2,3,2]{2,1,0:T(4,128)} custom-call(s32[2]{0:T(128)} %copy-done.11, bf16[8,2,48,1536]{3,2,1,0:T(8,128)(2,1)} %all-to-all-done.refs_1_.tau_ref, bf16[3,192,384]{2,1,0:T(8,128)(2,1)} %copy-done.5, bf16[3,192,384]{2,1,0:T(8,128)(2,1)} %copy-done.4, bf16[2,3,192,384]{3,2,1,0:T(8,128)(2,1)} %copy-done.1), custom_call_target="tpu_custom_call" | custom-call | flops 5435817984 | bytes 4128768 | tf_op jit(solution)/shard_map/pallas_call | solution.py:147
  100.5 4.6 %collective-permute-start.8 = (f32[2,3,2]{2,1,0:T(4,128)}, f32[2,3,2]{2,1,0:T(4,128)S(1)}, u32[]{:S(2)}, u32[]{:S(2)}) collective-permute-start(f32[2,3,2]{2,1,0:T(4,128)} %shard_map.50.refs_3_), channel_id=1, source_target_pairs={{0,8},{1,9},{2,10},{3,11},{4,12},{5,13},{6,14},{7,15},{8,0},{9,1},... | collective-permute-start | bytes 152 | tf_op jit(solution)/shard_map/ppermute | solution.py:18
  105.1 16.5 %collective-permute-done.7.refs_1_ = bf16[3,192,384]{2,1,0:T(8,128)(2,1)S(1)} collective-permute-done((bf16[3,192,384]{2,1,0:T(8,128)(2,1)S(1)}, bf16[3,192,384]{2,1,0:T(8,128)(2,1)S(1)}, u32[]{:S(2)}, u32[]{:S(2)}) %collective-permute-start.7) | collective-permute-done | bytes 442400 | tf_op jit(solution)/shard_map/ppermute | solution.py:23
  121.6 0.8 copy-done.12
  122.4 10.7 %collective-permute-done.6.refs_0_ = bf16[3,192,384]{2,1,0:T(8,128)(2,1)} collective-permute-done((bf16[3,192,384]{2,1,0:T(8,128)(2,1)S(1)}, bf16[3,192,384]{2,1,0:T(8,128)(2,1)}, u32[]{:S(2)}, u32[]{:S(2)}) %collective-permute-start.6) | collective-permute-done | bytes 442400 | tf_op jit(solution)/shard_map/ppermute | solution.py:23
  133.1 0.0 all-to-all-done.1.tau_ref
  133.1 15.4 %shard_map.51 = f32[2,3,2]{2,1,0:T(4,128)} custom-call(s32[2]{0:T(128)} %counts_ref.1, bf16[8,2,48,1536]{3,2,1,0:T(8,128)(2,1)} %all-to-all-done.1.tau_ref, bf16[3,192,384]{2,1,0:T(8,128)(2,1)} %collective-permute-done.6.refs_0_, bf16[3,192,384]{2,1,0:T(8,128)(2,1)} %copy-done.12, bf16[2,3,192,384]{3,2,1,0:T(8,128)(2,1)} %bitcast.15, ...), custom_call_target="tpu_custom_call" | custom-call | flops 5435817984 | bytes 4128768 | tf_op jit(solution)/shard_map/pallas_call | solution.py:147
  148.5 0.0 collective-permute-done.8
  148.5 0.7 add_multiply_fusion
  149.2 0.7 copy.8
  (17 shorter events, 0.1 us)
Async XLA Ops:
  0.0 16.8 %copy-start = (bf16[1,16,192,384]{3,2,1,0:T(8,128)(2,1)S(1)}, bf16[1,16,192,384]{3,2,1,0:T(8,128)(2,1)}, u32[]{:S(2)}) copy-start(bf16[1,16,192,384]{3,2,1,0:T(8,128)(2,1)} %param.5) | copy-start | bytes 7077892
  0.8 10.3 %collective-permute-start.2 = (s32[3]{0:T(128)S(1)}, s32[3]{0:T(128)S(1)}, u32[]{:S(2)}, u32[]{:S(2)}) collective-permute-start(s32[3]{0:T(128)S(1)} %get-tuple-element.5), channel_id=1, source_target_pairs={{0,10},{1,11},{2,12},{3,13},{4,14},{5,15},{6,0},{7,1},{8,2},{9,3},... | collective-permute-start | bytes 44 | tf_op jit(solution)/shard_map/ppermute | solution.py:23
  5.8 5.3 %collective-permute-start.1 = (s32[3]{0:T(128)S(1)}, s32[3]{0:T(128)S(1)}, u32[]{:S(2)}, u32[]{:S(2)}) collective-permute-start(s32[3]{0:T(128)S(1)} %get-tuple-element.6), channel_id=1, source_target_pairs={{0,5},{1,6},{2,7},{3,8},{4,9},{5,10},{6,11},{7,12},{8,13},{9,14},{... | collective-permute-start | bytes 44 | tf_op jit(solution)/shard_map/ppermute | solution.py:23
  6.6 4.6 %collective-permute-start = (s32[2]{0:T(128)}, s32[2]{0:T(128)S(1)}, u32[]{:S(2)}, u32[]{:S(2)}) collective-permute-start(s32[2]{0:T(128)} %counts_ref.1), channel_id=1, source_target_pairs={{0,8},{1,9},{2,10},{3,11},{4,12},{5,13},{6,14},{7,15},{8,0},{9,1},... | collective-permute-start | bytes 32 | tf_op jit(solution)/shard_map/ppermute | solution.py:18
  11.2 0.5 copy-start.11
  11.2 0.5 copy-start.7
  11.7 0.5 copy-start.9
  12.2 4.5 %copy-start.6 = (s32[2,3,2]{1,2,0:T(2,128)S(1)}, s32[2,3,2]{1,2,0:T(2,128)}, u32[]{:S(2)}) copy-start(s32[2,3,2]{1,2,0:T(2,128)} %param.6) | copy-start | bytes 148
  12.2 7.8 %copy-start.10 = (s32[3]{0:T(128)S(1)}, s32[3]{0:T(128)}, u32[]{:S(2)}) copy-start(s32[3]{0:T(128)} %copy-done.9) | copy-start | bytes 40
  12.2 67.8 %all-to-all-start = ((bf16[8,2,48,1536]{3,2,1,0:T(8,128)(2,1)}), bf16[8,2,48,1536]{3,2,1,0:T(8,128)(2,1)}, u32[]{:S(2)}, u32[]{:S(2)}) async-start(bf16[8,2,48,1536]{3,2,1,0:T(8,128)(2,1)} %shard_map.48), calls=%async_computation | async-start | bytes 4718592 | tf_op jit(solution)/shard_map/all_to_all | solution.py:192
  16.7 4.6 %copy-start.8 = (s32[3]{0:T(128)S(1)}, s32[3]{0:T(128)}, u32[]{:S(2)}) copy-start(s32[3]{0:T(128)} %copy-done.7) | copy-start | bytes 40
  18.5 61.6 %collective-permute-start.3 = (bf16[2,3,192,384]{3,2,1,0:T(8,128)(2,1)}, bf16[2,3,192,384]{3,2,1,0:T(8,128)(2,1)S(1)}, u32[]{:S(2)}, u32[]{:S(2)}) collective-permute-start(bf16[2,3,192,384]{3,2,1,0:T(8,128)(2,1)} %bitcast.14), channel_id=1, source_target_pairs={{0,8},{1,9},{2,10},{3,11},{4,12},{5,13},{6,14},{7,15},{8,0},{9,1},... | collective-permute-start | bytes 2654216 | tf_op jit(solution)/shard_map/ppermute | solution.py:18
  22.8 49.1 %collective-permute-start.5 = (bf16[3,192,384]{2,1,0:T(8,128)(2,1)}, bf16[3,192,384]{2,1,0:T(8,128)(2,1)S(1)}, u32[]{:S(2)}, u32[]{:S(2)}) collective-permute-start(bf16[3,192,384]{2,1,0:T(8,128)(2,1)} %gather_fusion.2), channel_id=1, source_target_pairs={{0,14},{1,15},{2,0},{3,1},{4,2},{5,3},{6,4},{7,5},{8,6},{9,7},{10,... | collective-permute-start | bytes 1327112 | tf_op jit(solution)/shard_map/ppermute | solution.py:23
  26.4 52.8 %collective-permute-start.4 = (bf16[3,192,384]{2,1,0:T(8,128)(2,1)}, bf16[3,192,384]{2,1,0:T(8,128)(2,1)S(1)}, u32[]{:S(2)}, u32[]{:S(2)}) collective-permute-start(bf16[3,192,384]{2,1,0:T(8,128)(2,1)} %gather_fusion.1), channel_id=1, source_target_pairs={{0,3},{1,4},{2,5},{3,6},{4,7},{5,8},{6,9},{7,10},{8,11},{9,12},{10... | collective-permute-start | bytes 1327112 | tf_op jit(solution)/shard_map/ppermute | solution.py:23
  71.9 0.8 copy-start.4
  79.2 0.8 copy-start.5
  80.0 1.0 copy-start.1
  81.0 4.5 %copy-start.3 = (bf16[3,192,384]{2,1,0:T(8,128)(2,1)S(1)}, bf16[3,192,384]{2,1,0:T(8,128)(2,1)}, u32[]{:S(2)}) copy-start(bf16[3,192,384]{2,1,0:T(8,128)(2,1)} %gather_fusion.2) | copy-start | bytes 1327108
  81.0 7.4 %copy-start.2 = (bf16[3,192,384]{2,1,0:T(8,128)(2,1)S(1)}, bf16[3,192,384]{2,1,0:T(8,128)(2,1)}, u32[]{:S(2)}) copy-start(bf16[3,192,384]{2,1,0:T(8,128)(2,1)} %gather_fusion.1) | copy-start | bytes 1327108
  81.0 52.1 %all-to-all-start.1 = ((bf16[8,2,48,1536]{3,2,1,0:T(8,128)(2,1)}), bf16[8,2,48,1536]{3,2,1,0:T(8,128)(2,1)}, u32[]{:S(2)}, u32[]{:S(2)}) async-start(bf16[8,2,48,1536]{3,2,1,0:T(8,128)(2,1)} %shard_map.49), calls=%async_computation.1 | async-start | bytes 4718592 | tf_op jit(solution)/shard_map/all_to_all | solution.py:192
  85.5 36.1 %collective-permute-start.7 = (bf16[3,192,384]{2,1,0:T(8,128)(2,1)S(1)}, bf16[3,192,384]{2,1,0:T(8,128)(2,1)S(1)}, u32[]{:S(2)}, u32[]{:S(2)}) collective-permute-start(bf16[3,192,384]{2,1,0:T(8,128)(2,1)S(1)} %copy-done.3), channel_id=1, source_target_pairs={{0,6},{1,7},{2,8},{3,9},{4,10},{5,11},{6,12},{7,13},{8,14},{9,15},... | collective-permute-start | bytes 1327112 | tf_op jit(solution)/shard_map/ppermute | solution.py:23
  88.3 44.7 %collective-permute-start.6 = (bf16[3,192,384]{2,1,0:T(8,128)(2,1)S(1)}, bf16[3,192,384]{2,1,0:T(8,128)(2,1)}, u32[]{:S(2)}, u32[]{:S(2)}) collective-permute-start(bf16[3,192,384]{2,1,0:T(8,128)(2,1)S(1)} %copy-done.2), channel_id=1, source_target_pairs={{0,11},{1,12},{2,13},{3,14},{4,15},{5,0},{6,1},{7,2},{8,3},{9,4},{... | collective-permute-start | bytes 1327112 | tf_op jit(solution)/shard_map/ppermute | solution.py:23
  100.5 48.0 %collective-permute-start.8 = (f32[2,3,2]{2,1,0:T(4,128)}, f32[2,3,2]{2,1,0:T(4,128)S(1)}, u32[]{:S(2)}, u32[]{:S(2)}) collective-permute-start(f32[2,3,2]{2,1,0:T(4,128)} %shard_map.50.refs_3_), channel_id=1, source_target_pairs={{0,8},{1,9},{2,10},{3,11},{4,12},{5,13},{6,14},{7,15},{8,0},{9,1},... | collective-permute-start | bytes 152 | tf_op jit(solution)/shard_map/ppermute | solution.py:18
  121.6 0.8 copy-start.12

commit v4 on v2

--- a/solution.py
+++ b/solution.py
@@ -9,7 +9,9 @@
 
 NT_DIMS = (((1,), (1,)), ((), ()))
 ANYWHERE = pl.BlockSpec(memory_space=pl.ANY)
+VMEM_BYTES = 56 * 1024 * 1024
 HBM = pl.BlockSpec(memory_space=pltpu.HBM)
+VMEM = pl.BlockSpec(memory_space=pltpu.VMEM)
 SMEM = pl.BlockSpec(memory_space=pltpu.SMEM)
 
 
@@ -46,11 +48,34 @@
     return pl.pallas_call(
         regroup_kernel,
         in_specs=[SMEM, HBM],
-        out_specs=pl.BlockSpec(memory_space=pltpu.VMEM),
+        out_specs=VMEM,
         out_shape=jax.ShapeDtypeStruct((half, 2, pair_count, columns, width), perambulator.dtype),
         scratch_shapes=[pltpu.SemaphoreType.DMA((2 * half,))],
-        compiler_params=pltpu.CompilerParams(vmem_limit_bytes=56 * 1024 * 1024),
+        compiler_params=pltpu.CompilerParams(vmem_limit_bytes=58 * 1024 * 1024),
     )(high.reshape(1), source)
+
+
+def select_kernel(index_ref, set_ref, out_ref, sems):
+    copies = [
+        pltpu.make_async_copy(
+            set_ref.at[jnp.clip(index_ref[i], 0, set_ref.shape[0] - 1)], out_ref.at[i], sems.at[i]
+        )
+        for i in range(out_ref.shape[0])
+    ]
+    for copy in copies:
+        copy.start()
+    for copy in copies:
+        copy.wait()
+
+
+def selected(elementals, index):
+    return pl.pallas_call(
+        select_kernel,
+        in_specs=[SMEM, ANYWHERE],
+        out_specs=VMEM,
+        out_shape=jax.ShapeDtypeStruct(index.shape + elementals.shape[1:], elementals.dtype),
+        scratch_shapes=[pltpu.SemaphoreType.DMA(index.shape)],
+    )(index, elementals)
 
 
 def tied(x, *earlier):
@@ -68,9 +93,9 @@
     return jnp.concatenate([x[:, vectors:], x[:, :vectors]], axis=1)
 
 
-def pairs_kernel(pair_count, counts_ref, tau_ref, *refs):
-    sink_refs = refs[: 2 * pair_count]
-    source_refs = refs[2 * pair_count : 2 * pair_count + 2]
+def pairs_kernel(pairs, scale, counts_ref, begin_ref, tau_ref, *refs):
+    sink_refs = refs[:pairs]
+    source_ref = refs[pairs]
     out_ref, sinks, sources, swap_ref, left_ref, sink_sems, source_sems = refs[-7:]
     slots, vectors, packed = sinks.shape[1:]
     spins, _, width = swap_ref.shape
@@ -81,11 +106,10 @@
 
     @pl.when(pair == 0)
     def _():
-        for p in range(2 * pair_count):
-            side, slot = divmod(p, pair_count)
+        for p in range(pairs):
             for d in range(slots):
-                out_ref[p, d, 0] = 0.0
-                out_ref[p, d, 1] = 0.0
+                out_ref[p, d, 0] = begin_ref[p, d, 0] * scale
+                out_ref[p, d, 1] = begin_ref[p, d, 1] * scale
 
                 @pl.when(d < counts_ref[p])
                 def _():
@@ -93,7 +117,7 @@
                         sink_refs[p].at[d], sinks.at[p, d], sink_sems.at[p, d]
                     ).start()
                     pltpu.make_async_copy(
-                        source_refs[side].at[slot, d], sources.at[p, d], source_sems.at[p, d]
+                        source_ref.at[p, d], sources.at[p, d], source_sems.at[p, d]
                     ).start()
 
     def tile(s):
@@ -137,16 +161,16 @@
                 left_ref[s], swap_ref[s], NT_DIMS, preferred_element_type=jnp.float32
             )
         pltpu.make_async_copy(
-            source_refs[0].at[0, 0], sources.at[pair, d], source_sems.at[pair, d]
+            source_ref.at[0, 0], sources.at[pair, d], source_sems.at[pair, d]
         ).wait()
         source = sources[pair, d].astype(jnp.float32)
         real = source[:, :vectors]
         imag = source[:, vectors:]
-        out_ref[pair, d, 0] = jnp.sum(real * block_real - imag * block_imag)
-        out_ref[pair, d, 1] = jnp.sum(real * block_imag + imag * block_real)
-
-
-def pairs_sums(tau, sinks, sources, counts):
+        out_ref[pair, d, 0] += jnp.sum(real * block_real - imag * block_imag) * scale
+        out_ref[pair, d, 1] += jnp.sum(real * block_imag + imag * block_real) * scale
+
+
+def pairs_sums(tau, first, sinks, sources, counts, begin, scale):
     pairs = len(sinks)
     slots, vectors, packed = sinks[0].shape
     pieces, _, columns, width = tau.shape
@@ -154,10 +178,14 @@
     flops = 4 * pairs * spins * slots * width * vectors * packed
     moved = 2 * pairs * (spins * vectors * width + 2 * slots * vectors * packed)
     return pl.pallas_call(
-        functools.partial(pairs_kernel, pairs // 2),
+        functools.partial(pairs_kernel, pairs, scale),
         grid=(pairs,),
-        in_specs=[SMEM, pl.BlockSpec((pieces, 1, columns, width), lambda p: (0, p, 0, 0))]
-        + [HBM] * (pairs + 2),
+        in_specs=[
+            SMEM,
+            SMEM,
+            pl.BlockSpec((pieces, 1, columns, width), lambda p: (0, first + p, 0, 0)),
+        ]
+        + [HBM] * (pairs + 1),
         out_specs=SMEM,
         out_shape=jax.ShapeDtypeStruct((pairs, slots, 2), jnp.float32),
         scratch_shapes=[
@@ -168,9 +196,9 @@
             pltpu.SemaphoreType.DMA((pairs, slots)),
             pltpu.SemaphoreType.DMA((pairs, slots)),
         ],
-        compiler_params=pltpu.CompilerParams(vmem_limit_bytes=56 * 1024 * 1024),
+        compiler_params=pltpu.CompilerParams(vmem_limit_bytes=VMEM_BYTES),
         cost_estimate=pl.CostEstimate(flops=flops, bytes_accessed=moved, transcendentals=0),
-    )(counts, tau, *sinks, *sources)
+    )(counts, begin, tau, *sinks, sources)
 
 
 def body(perambulator, elementals, diagrams, counts):
@@ -187,12 +215,14 @@
     steps = [(slot + 1) * devices // (pair_count + 1) for slot in range(pair_count)]
     wanted = [passed_along(diagrams[slot, :, 0], by) for slot, by in enumerate(steps)]
     given_counts = exchanged(counts, half)
-    own_sources = jnp.take(own_set, diagrams[:, :, 1].reshape(-1), axis=0, mode="clip")
+    own_sources = selected(own_set, diagrams[:, :, 1].reshape(-1))
     own_sources = own_sources.reshape(pair_count, slots, vectors, packed)
     given_sources = exchanged(own_sources, half)
-    chosen = [jnp.take(own_set, index, axis=0, mode="clip") for index in wanted]
+    chosen = [selected(own_set, index) for index in wanted]
     given_sinks = [passed_along(sets, -by, half) for by, sets in zip(steps, chosen)]
-    own_sinks = [passed_along(sets, -by) for by, sets in zip(steps, chosen)]
+    own_sinks = [
+        passed_along(tied(sets, sent), -by) for by, sets, sent in zip(steps, chosen, given_sinks)
+    ]
 
     tau = lax.all_to_all(
         tied(regrouped(perambulator, high, half, pair_count), given_counts, *wanted),
@@ -206,14 +236,11 @@
         tau = jnp.moveaxis(tau, 1, 0).reshape(2 * pair_count, -1, vectors, width)
         tau = jnp.moveaxis(tau, 0, 1)
 
-    sums = pairs_sums(
-        tau,
-        given_sinks + own_sinks,
-        (given_sources, own_sources),
-        jnp.concatenate([given_counts, counts]),
-    )
-    got = exchanged(sums[:pair_count], half)
-    return (sums[pair_count:] + got) / (columns * devices)
+    zeros = jnp.zeros((pair_count, slots, 2), jnp.float32)
+    given = pairs_sums(tau, 0, given_sinks, given_sources, given_counts, zeros, 1.0)
+    got = exchanged(given, half)
+    scale = 1.0 / (columns * devices)
+    return pairs_sums(tau, pair_count, own_sinks, own_sources, counts, got, scale)
 
 
 def solution(mesh):

time: 152 us -> 148 us (0.974)
  the two profiles are of different devices: /device:TPU:5 before, /device:TPU:1 now
where the time goes in v4:
time: 148 us; the launch traced here: 145 us
  waiting for transfers between devices  79.3 us (54%)
  Pallas kernels  31.3 us (21%)
  starting transfers between devices  26.7 us (18%)
  local copies, waits for them, and re-layouts  7.44 us (5%)
    ppermute x6, waiting for transfers between devices, passed_along(): lax.ppermute(x, 'tm', [(i, (i + by) % devices ^ mask) for i in range(devi...  79.3 us
    pallas_call x2, Pallas kernels, pairs_sums(): pl.pallas_call(functools.partial(pairs_kernel, pairs, scale), grid=(pairs...  18.8 us
    ppermute x3, starting transfers between devices, exchanged(): return lax.ppermute(x, 'tm', [(i, i ^ mask) for i in range(devices)])  11.3 us
    ppermute x6, starting transfers between devices, passed_along(): lax.ppermute(x, 'tm', [(i, (i + by) % devices ^ mask) for i in range(devi...  10.7 us
    pallas_call x3, Pallas kernels, selected(): pl.pallas_call(select_kernel, in_specs=[SMEM, ANYWHERE], out_specs=VMEM,...  7.92 us
    all_to_all x1, starting transfers between devices, body(): lax.all_to_all(tied(regrouped(perambulator, high, half, pair_count), give...  4.69 us
    pallas_call x1, Pallas kernels, regrouped(): pl.pallas_call(regroup_kernel, in_specs=[SMEM, HBM], out_specs=VMEM, out_...  4.61 us
    unnamed x20, local copies, waits for them, and re-layouts  4.16 us
  transfers between devices with their start and end apart: 10, of which 2 were waited for; matrix products, arithmetic and copies ran while one was open for 1% of the time, Pallas kernels for 14%

profile of v4, /device:TPU:1, one launch (start us, length us, event | category | flops | bytes accessed | tf_op | source)
XLA Modules:
  0.0 144.8 jit_solution(2469768125337885607)
XLA Ops:
  0.0 0.7 slice_bitcast_fusion
  0.7 3.6 %collective-permute-start.1 = (s32[3]{0:T(128)S(1)}, s32[3]{0:T(128)S(1)}, u32[]{:S(2)}, u32[]{:S(2)}) collective-permute-start(s32[3]{0:T(128)S(1)} %get-tuple-element.6), channel_id=1, source_target_pairs={{0,5},{1,6},{2,7},{3,8},{4,9},{5,10},{6,11},{7,12},{8,13},{9,14},{... | collective-permute-start | bytes 44 | tf_op jit(solution)/shard_map/ppermute | solution.py:25
  4.3 0.5 collective-permute-start.2
  4.8 2.9 %collective-permute-start = (s32[2]{0:T(128)}, s32[2]{0:T(128)S(1)}, u32[]{:S(2)}, u32[]{:S(2)}) collective-permute-start(s32[2]{0:T(128)} %counts_ref.1), channel_id=1, source_target_pairs={{0,8},{1,9},{2,10},{3,11},{4,12},{5,13},{6,14},{7,15},{8,0},{9,1},... | collective-permute-start | bytes 32 | tf_op jit(solution)/shard_map/ppermute | solution.py:20
  7.7 4.6 %shard_map.46.refs_0_ = bf16[8,2,2,48,1536]{4,3,2,1,0:T(8,128)(2,1)} custom-call(s32[1]{0:T(128)} %bitcast.high_ref, bf16[2,8,2,48,1536]{4,3,2,1,0:T(8,128)(2,1)} %bitcast.12), custom_call_target="tpu_custom_call" | custom-call | tf_op jit(solution)/shard_map/pallas_call | solution.py:48
  12.3 0.0 collective-permute-done.refs_1_.counts_ref
  12.3 0.0 copy-start.5
  12.3 0.0 collective-permute-done.1.refs_2_.index_ref
  12.3 0.0 copy-start.3
  12.3 0.0 collective-permute-done.2.refs_3_.index_ref
  12.3 0.5 copy-done.5
  12.8 0.0 copy-done.3
  12.8 0.0 copy-start.2
  12.8 0.5 copy-done.2
  13.3 0.0 copy-start.4
  13.3 4.7 %all-to-all-start = ((bf16[8,2,2,48,1536]{4,3,2,1,0:T(8,128)(2,1)}), bf16[8,2,2,48,1536]{4,3,2,1,0:T(8,128)(2,1)}, u32[]{:S(2)}, u32[]{:S(2)}) async-start(bf16[8,2,2,48,1536]{4,3,2,1,0:T(8,128)(2,1)} %shard_map.47), calls=%async_computation | async-start | bytes 9437184 | tf_op jit(solution)/shard_map/all_to_all | solution.py:227
  18.0 0.0 copy-done.4
  18.1 0.6 reshape_squeeze.3.index_ref
  18.6 2.9 %shard_map.50 = bf16[6,192,384]{2,1,0:T(8,128)(2,1)} custom-call(s32[6]{0:T(128)} %reshape_squeeze.3.index_ref, bf16[16,192,384]{2,1,0:T(8,128)(2,1)} %bitcast.9), custom_call_target="tpu_custom_call" | custom-call | tf_op jit(solution)/shard_map/pallas_call | solution.py:72
  21.5 1.7 %collective-permute-start.5 = (bf16[2,3,192,384]{3,2,1,0:T(8,128)(2,1)}, bf16[2,3,192,384]{3,2,1,0:T(8,128)(2,1)S(1)}, u32[]{:S(2)}, u32[]{:S(2)}) collective-permute-start(bf16[2,3,192,384]{3,2,1,0:T(8,128)(2,1)} %bitcast.13), channel_id=1, source_target_pairs={{0,8},{1,9},{2,10},{3,11},{4,12},{5,13},{6,14},{7,15},{8,0},{9,1},... | collective-permute-start | bytes 2654216 | tf_op jit(solution)/shard_map/ppermute | solution.py:20
  23.2 2.5 %shard_map.48.refs_0_ = bf16[3,192,384]{2,1,0:T(8,128)(2,1)} custom-call(s32[3]{0:T(128)} %copy-done.3, bf16[16,192,384]{2,1,0:T(8,128)(2,1)} %bitcast.10), custom_call_target="tpu_custom_call" | custom-call | tf_op jit(solution)/shard_map/pallas_call | solution.py:72
  25.7 2.0 %collective-permute-start.3 = (bf16[3,192,384]{2,1,0:T(8,128)(2,1)}, bf16[3,192,384]{2,1,0:T(8,128)(2,1)S(1)}, u32[]{:S(2)}, u32[]{:S(2)}) collective-permute-start(bf16[3,192,384]{2,1,0:T(8,128)(2,1)} %shard_map.48.refs_0_), channel_id=1, source_target_pairs={{0,3},{1,4},{2,5},{3,6},{4,7},{5,8},{6,9},{7,10},{8,11},{9,12},{10... | collective-permute-start | bytes 1327112 | tf_op jit(solution)/shard_map/ppermute | solution.py:25
  27.7 2.5 %shard_map.49.refs_0_ = bf16[3,192,384]{2,1,0:T(8,128)(2,1)} custom-call(s32[3]{0:T(128)} %copy-done.2, bf16[16,192,384]{2,1,0:T(8,128)(2,1)} %bitcast.11), custom_call_target="tpu_custom_call" | custom-call | tf_op jit(solution)/shard_map/pallas_call | solution.py:72
  30.3 3.0 %collective-permute-start.4 = (bf16[3,192,384]{2,1,0:T(8,128)(2,1)}, bf16[3,192,384]{2,1,0:T(8,128)(2,1)S(1)}, u32[]{:S(2)}, u32[]{:S(2)}) collective-permute-start(bf16[3,192,384]{2,1,0:T(8,128)(2,1)} %shard_map.49.refs_0_), channel_id=1, source_target_pairs={{0,14},{1,15},{2,0},{3,1},{4,2},{5,3},{6,4},{7,5},{8,6},{9,7},{10,... | collective-permute-start | bytes 1327112 | tf_op jit(solution)/shard_map/ppermute | solution.py:25
  33.3 68.7 %collective-permute-done.3.refs_0_.refs_1_ = bf16[3,192,384]{2,1,0:T(8,128)(2,1)S(1)} collective-permute-done((bf16[3,192,384]{2,1,0:T(8,128)(2,1)}, bf16[3,192,384]{2,1,0:T(8,128)(2,1)S(1)}, u32[]{:S(2)}, u32[]{:S(2)}) %collective-permute-start.3) | collective-permute-done | bytes 442400 | tf_op jit(solution)/shard_map/ppermute | solution.py:25
  102.0 0.0 copy-start
  102.0 0.8 copy-done
  102.8 0.0 collective-permute-start.7
  102.8 0.0 collective-permute-done.4.refs_1_
  102.8 0.0 copy-start.1
  102.8 0.8 copy-done.1
  103.5 1.6 %collective-permute-start.8 = (bf16[3,192,384]{2,1,0:T(8,128)(2,1)}, bf16[3,192,384]{2,1,0:T(8,128)(2,1)S(1)}, u32[]{:S(2)}, u32[]{:S(2)}) collective-permute-start(bf16[3,192,384]{2,1,0:T(8,128)(2,1)} %shard_map.53), channel_id=1, source_target_pairs={{0,6},{1,7},{2,8},{3,9},{4,10},{5,11},{6,12},{7,13},{8,14},{9,15},... | collective-permute-start | bytes 1327112 | tf_op jit(solution)/shard_map/ppermute | solution.py:25
  105.1 0.0 collective-permute-done.5.refs_2_
  105.1 0.0 copy-start.6
  105.1 0.0 all-to-all-done
  105.1 0.7 broadcast_1_begin_ref.2.begin_ref
  105.8 0.2 copy-done.6
  106.0 7.4 %shard_map.51 = f32[2,3,2]{2,1,0:T(4,128)} custom-call(s32[2]{0:T(128)} %copy-done.5, f32[2,3,2]{2,1,0:T(4,128)} %broadcast_1_begin_ref.2.begin_ref, bf16[8,4,48,1536]{3,2,1,0:T(8,128)(2,1)} %bitcast.4.tau_ref, bf16[3,192,384]{2,1,0:T(8,128)(2,1)} %copy-done, bf16[3,192,384]{2,1,0:T(8,128)(2,1)} %copy-done.1, bf16[2,3,192,384]{3,2,1,0:T(8,128)(2,1)} %copy-done.6), custom_call_target="tpu_custom_call" | custom-call | flops 5435817984 | bytes 4128768 | tf_op jit(solution)/shard_map/pallas_call | solution.py:180
  113.4 6.7 %collective-permute-start.6 = (f32[2,3,2]{2,1,0:T(4,128)}, f32[2,3,2]{2,1,0:T(4,128)S(1)}, u32[]{:S(2)}, u32[]{:S(2)}) collective-permute-start(f32[2,3,2]{2,1,0:T(4,128)} %shard_map.51), channel_id=1, source_target_pairs={{0,8},{1,9},{2,10},{3,11},{4,12},{5,13},{6,14},{7,15},{8,0},{9,1},... | collective-permute-start | bytes 152 | tf_op jit(solution)/shard_map/ppermute | solution.py:20
  120.2 0.0 collective-permute-done.7.refs_0_
  120.2 0.0 copy-start.7
  120.2 10.5 %collective-permute-done.8.refs_1_ = bf16[3,192,384]{2,1,0:T(8,128)(2,1)S(1)} collective-permute-done((bf16[3,192,384]{2,1,0:T(8,128)(2,1)}, bf16[3,192,384]{2,1,0:T(8,128)(2,1)S(1)}, u32[]{:S(2)}, u32[]{:S(2)}) %collective-permute-start.8) | collective-permute-done | bytes 442400 | tf_op jit(solution)/shard_map/ppermute | solution.py:25
  130.7 0.0 collective-permute-done.6.begin_ref
  130.7 0.0 copy-done.7
  130.7 0.8 copy-done.8
  131.5 0.6 copy-done.9
  132.1 11.4 %shard_map.54 = f32[2,3,2]{2,1,0:T(4,128)} custom-call(s32[2]{0:T(128)} %counts_ref.1, f32[2,3,2]{2,1,0:T(4,128)} %copy-done.9, bf16[8,4,48,1536]{3,2,1,0:T(8,128)(2,1)} %bitcast.4.tau_ref, bf16[3,192,384]{2,1,0:T(8,128)(2,1)} %copy-done.7, bf16[3,192,384]{2,1,0:T(8,128)(2,1)} %copy-done.8, bf16[2,3,192,384]{3,2,1,0:T(8,128)(2,1)} %bitcast.14), custom_call_target="tpu_custom_call" | custom-call | flops 5435817984 | bytes 4128768 | tf_op jit(solution)/shard_map/pallas_call | solution.py:180
  143.5 1.3 copy.9
  (6 shorter events, 0.0 us)
Async XLA Ops:
  0.7 11.6 %collective-permute-start.1 = (s32[3]{0:T(128)S(1)}, s32[3]{0:T(128)S(1)}, u32[]{:S(2)}, u32[]{:S(2)}) collective-permute-start(s32[3]{0:T(128)S(1)} %get-tuple-element.6), channel_id=1, source_target_pairs={{0,5},{1,6},{2,7},{3,8},{4,9},{5,10},{6,11},{7,12},{8,13},{9,14},{... | collective-permute-start | bytes 44 | tf_op jit(solution)/shard_map/ppermute | solution.py:25
  4.3 8.0 %collective-permute-start.2 = (s32[3]{0:T(128)S(1)}, s32[3]{0:T(128)S(1)}, u32[]{:S(2)}, u32[]{:S(2)}) collective-permute-start(s32[3]{0:T(128)S(1)} %get-tuple-element.5), channel_id=1, source_target_pairs={{0,10},{1,11},{2,12},{3,13},{4,14},{5,15},{6,0},{7,1},{8,2},{9,3},... | collective-permute-start | bytes 44 | tf_op jit(solution)/shard_map/ppermute | solution.py:25
  4.8 7.5 %collective-permute-start = (s32[2]{0:T(128)}, s32[2]{0:T(128)S(1)}, u32[]{:S(2)}, u32[]{:S(2)}) collective-permute-start(s32[2]{0:T(128)} %counts_ref.1), channel_id=1, source_target_pairs={{0,8},{1,9},{2,10},{3,11},{4,12},{5,13},{6,14},{7,15},{8,0},{9,1},... | collective-permute-start | bytes 32 | tf_op jit(solution)/shard_map/ppermute | solution.py:20
  12.3 0.5 copy-start.5
  12.3 0.5 copy-start.3
  12.8 0.5 copy-start.2
  13.3 4.7 %copy-start.4 = (s32[2,3,2]{1,2,0:T(2,128)S(1)}, s32[2,3,2]{1,2,0:T(2,128)}, u32[]{:S(2)}) copy-start(s32[2,3,2]{1,2,0:T(2,128)} %param.6) | copy-start | bytes 148
  13.3 91.8 %all-to-all-start = ((bf16[8,2,2,48,1536]{4,3,2,1,0:T(8,128)(2,1)}), bf16[8,2,2,48,1536]{4,3,2,1,0:T(8,128)(2,1)}, u32[]{:S(2)}, u32[]{:S(2)}) async-start(bf16[8,2,2,48,1536]{4,3,2,1,0:T(8,128)(2,1)} %shard_map.47), calls=%async_computation | async-start | bytes 9437184 | tf_op jit(solution)/shard_map/all_to_all | solution.py:227
  21.5 83.6 %collective-permute-start.5 = (bf16[2,3,192,384]{3,2,1,0:T(8,128)(2,1)}, bf16[2,3,192,384]{3,2,1,0:T(8,128)(2,1)S(1)}, u32[]{:S(2)}, u32[]{:S(2)}) collective-permute-start(bf16[2,3,192,384]{3,2,1,0:T(8,128)(2,1)} %bitcast.13), channel_id=1, source_target_pairs={{0,8},{1,9},{2,10},{3,11},{4,12},{5,13},{6,14},{7,15},{8,0},{9,1},... | collective-permute-start | bytes 2654216 | tf_op jit(solution)/shard_map/ppermute | solution.py:20
  25.7 76.3 %collective-permute-start.3 = (bf16[3,192,384]{2,1,0:T(8,128)(2,1)}, bf16[3,192,384]{2,1,0:T(8,128)(2,1)S(1)}, u32[]{:S(2)}, u32[]{:S(2)}) collective-permute-start(bf16[3,192,384]{2,1,0:T(8,128)(2,1)} %shard_map.48.refs_0_), channel_id=1, source_target_pairs={{0,3},{1,4},{2,5},{3,6},{4,7},{5,8},{6,9},{7,10},{8,11},{9,12},{10... | collective-permute-start | bytes 1327112 | tf_op jit(solution)/shard_map/ppermute | solution.py:25
  30.3 72.5 %collective-permute-start.4 = (bf16[3,192,384]{2,1,0:T(8,128)(2,1)}, bf16[3,192,384]{2,1,0:T(8,128)(2,1)S(1)}, u32[]{:S(2)}, u32[]{:S(2)}) collective-permute-start(bf16[3,192,384]{2,1,0:T(8,128)(2,1)} %shard_map.49.refs_0_), channel_id=1, source_target_pairs={{0,14},{1,15},{2,0},{3,1},{4,2},{5,3},{6,4},{7,5},{8,6},{9,7},{10,... | collective-permute-start | bytes 1327112 | tf_op jit(solution)/shard_map/ppermute | solution.py:25
  102.0 0.8 copy-start
  102.8 17.4 %collective-permute-start.7 = (bf16[3,192,384]{2,1,0:T(8,128)(2,1)}, bf16[3,192,384]{2,1,0:T(8,128)(2,1)S(1)}, u32[]{:S(2)}, u32[]{:S(2)}) collective-permute-start(bf16[3,192,384]{2,1,0:T(8,128)(2,1)} %shard_map.52), channel_id=1, source_target_pairs={{0,11},{1,12},{2,13},{3,14},{4,15},{5,0},{6,1},{7,2},{8,3},{9,4},{... | collective-permute-start | bytes 1327112 | tf_op jit(solution)/shard_map/ppermute | solution.py:25
  102.8 0.8 copy-start.1
  103.5 27.2 %collective-permute-start.8 = (bf16[3,192,384]{2,1,0:T(8,128)(2,1)}, bf16[3,192,384]{2,1,0:T(8,128)(2,1)S(1)}, u32[]{:S(2)}, u32[]{:S(2)}) collective-permute-start(bf16[3,192,384]{2,1,0:T(8,128)(2,1)} %shard_map.53), channel_id=1, source_target_pairs={{0,6},{1,7},{2,8},{3,9},{4,10},{5,11},{6,12},{7,13},{8,14},{9,15},... | collective-permute-start | bytes 1327112 | tf_op jit(solution)/shard_map/ppermute | solution.py:25
  105.1 0.9 copy-start.6
  113.4 17.3 %collective-permute-start.6 = (f32[2,3,2]{2,1,0:T(4,128)}, f32[2,3,2]{2,1,0:T(4,128)S(1)}, u32[]{:S(2)}, u32[]{:S(2)}) collective-permute-start(f32[2,3,2]{2,1,0:T(4,128)} %shard_map.51), channel_id=1, source_target_pairs={{0,8},{1,9},{2,10},{3,11},{4,12},{5,13},{6,14},{7,15},{8,0},{9,1},... | collective-permute-start | bytes 152 | tf_op jit(solution)/shard_map/ppermute | solution.py:20
  120.2 10.5 %copy-start.7 = (bf16[3,192,384]{2,1,0:T(8,128)(2,1)}, bf16[3,192,384]{2,1,0:T(8,128)(2,1)S(1)}, u32[]{:S(2)}) copy-start(bf16[3,192,384]{2,1,0:T(8,128)(2,1)S(1)} %collective-permute-done.7.refs_0_) | copy-start | bytes 1327108
  130.7 0.8 copy-start.8
  131.5 0.6 copy-start.9
